TPU v7x, 32 devices: a whole 2x2x4 slice. The times are simulated.
32 devices in a mesh: bucket: 4 (over z), seq: 8 (over y, x, core).
Axes of the slice: x: 2, y: 2, z: 4, core: 2. Of those that a mesh axis runs over, the one named last changes fastest.
Arguments:
- frames: bfloat16 [4, 2048, 768], P('bucket', 'seq'), may hold values from -6 to 6
- w_qkv: bfloat16 [2, 768, 2304], replicated, may hold values from -0.21875 to 0.21875
- b_qv: float32 [2, 1536], replicated, may hold values from -3 to 3
- w_out: bfloat16 [2, 768, 768], replicated, may hold values from -0.875 to 0.875
- b_out: float32 [2, 768], replicated, may hold values from -3 to 3
- ln_gain: float32 [2, 2, 768], replicated, may hold values from 0.5 to 1.5
- ln_shift: float32 [2, 2, 768], replicated, may hold values from -3 to 3
- w_up: bfloat16 [2, 768, 3072], replicated, may hold values from -0.21875 to 0.21875
- b_up: float32 [2, 3072], replicated, may hold values from -3 to 3
- w_down: bfloat16 [2, 3072, 768], replicated, may hold values from -0.109375 to 0.109375
- b_down: float32 [2, 768], replicated, may hold values from -3 to 3
- cotangent: bfloat16 [4, 2048, 768], P('bucket', 'seq'), may hold values from -6 to 6
- clip_lengths: int32 [4, 8], P('bucket'), may hold values from 1 to 1917, as said below
- valid_lengths: int32 [4, 8], P('bucket'), may hold values from 1 to 1917, as said below
Outputs:
- activations: bfloat16 [4, 2048, 768], P('bucket', 'seq')
- input_grad: float32 [4, 2048, 768], P('bucket', 'seq')
- grad_w_qkv: float32 [2, 768, 2304], P(None, 'seq')
- grad_b_qv: float32 [2, 1536], P(None, 'seq')
- grad_w_out: float32 [2, 768, 768], P(None, 'seq')
- grad_b_out: float32 [2, 768], P(None, 'seq')
- grad_ln_gain: float32 [2, 2, 768], P(None, None, 'seq')
- grad_ln_shift: float32 [2, 2, 768], P(None, None, 'seq')
- grad_w_up: float32 [2, 768, 3072], P(None, 'seq')
- grad_b_up: float32 [2, 3072], P(None, 'seq')
- grad_w_down: float32 [2, 3072, 768], P(None, 'seq')
- grad_b_down: float32 [2, 768], P(None, 'seq')
Inputs may be any that keep to these rules, and one draw needn't show every extreme that they name: `clip_lengths`: the 8 lengths of a bucket sum to 2048; in every bucket one clip has exactly 1917 frames and runs from the first device of seq to the last; the others have at most 33 frames each. `valid_lengths`: at most the clip's length; the longest clip of a bucket has no padding.
All inputs are finite; a program needn't handle non-finite values.
Results may differ from a plain program's by a relative error of at most 0.038.
Values may be sent and summed in bfloat16 or wider, within the bound.
No kernel may reach another device: no remote copies, remote signals or barrier semaphores. Data moves between devices by JAX's collectives and lax.ppermute only.
A program may use at most 256 MiB of HBM per device.

v0:
```python
import jax
import jax.numpy as jnp
from jax import lax
from jax.sharding import PartitionSpec as P

HEADS = 12
LAYERS = 2


def clip_tags(lengths, valid, begin, count):
    position = begin + jnp.arange(count, dtype=jnp.int32)
    ends = jnp.cumsum(lengths)
    starts = ends - lengths
    inside = (position[:, None] >= starts[None, :]) & (position[:, None] < ends[None, :])
    labels = jnp.arange(lengths.shape[0], dtype=jnp.int32)
    segment = jnp.sum(jnp.where(inside, labels[None, :], 0), axis=1)
    live = jnp.any(inside & (position[:, None] < (starts + valid)[None, :]), axis=1)
    return (segment, jnp.where(live, segment, -1))


def layer_norm(hidden, gain, shift):
    center = hidden - jnp.mean(hidden, axis=-1, keepdims=True)
    spread = jnp.mean(center * center, axis=-1, keepdims=True)
    return center * lax.rsqrt(spread + 1e-05) * gain + shift


def exact_gelu(hidden):
    return jax.nn.gelu(hidden, approximate=False)


def split_heads(matrix):
    return matrix.reshape(matrix.shape[0], HEADS, -1)


def pair_terms(
    query_heads,
    grad_heads,
    log_total,
    correction,
    query_seg,
    key_heads,
    value_heads,
    key_tag,
    scale,
):
    scores = (
        jnp.einsum("qhd,khd->hqk", query_heads, key_heads, preferred_element_type=jnp.float32)
        * scale
    )
    allowed = (query_seg[:, None] == key_tag[None, :])[None]
    scores = jnp.where(allowed, scores, -1e30)
    probs = jnp.where(allowed, jnp.exp(scores - log_total[..., None]), 0.0)
    grad_probs = jnp.einsum(
        "qhd,khd->hqk", grad_heads, value_heads, preferred_element_type=jnp.float32
    )
    grad_scores = (probs * (grad_probs - correction[..., None])).astype(jnp.bfloat16)
    return (probs.astype(jnp.bfloat16), grad_scores)


def forward_layer(hidden, weights, query_seg, lengths, valid):
    w_qkv, b_qv, w_out, b_out, gain, shift, w_up, b_up, w_down, b_down = weights
    rows, width = hidden.shape
    scale = (width // HEADS) ** (-0.5)
    inputs = hidden.astype(jnp.bfloat16)
    projected = jnp.dot(inputs, w_qkv, preferred_element_type=jnp.float32)
    queries = (projected[:, :width] + b_qv[:width]).astype(jnp.bfloat16)
    keys = projected[:, width : 2 * width].astype(jnp.bfloat16)
    values = (projected[:, 2 * width :] + b_qv[width:]).astype(jnp.bfloat16)
    query_heads = split_heads(queries)
    initial = (
        jnp.full((HEADS, rows), -1e30, jnp.float32),
        jnp.zeros((HEADS, rows), jnp.float32),
        jnp.zeros((HEADS, rows, width // HEADS), jnp.float32),
    )
    key_piece = lax.all_gather(keys, "seq", axis=0, tiled=True)
    value_piece = lax.all_gather(values, "seq", axis=0, tiled=True)
    count = key_piece.shape[0] // rows
    key_blocks = key_piece.reshape(count, rows, HEADS, -1)
    value_blocks = value_piece.reshape(count, rows, HEADS, -1)

    def fold_inner(state, item):
        key_heads, value_heads, block_at = item
        _, block_tag = clip_tags(lengths, valid, block_at * rows, rows)
        running, denominator, weighted = state
        scores = (
            jnp.einsum("qhd,khd->hqk", query_heads, key_heads, preferred_element_type=jnp.float32)
            * scale
        )
        allowed = (query_seg[:, None] == block_tag[None, :])[None]
        scores = jnp.where(allowed, scores, -1e30)
        raised = jnp.maximum(running, jnp.max(scores, axis=-1))
        block_probs = jnp.where(allowed, jnp.exp(scores - raised[..., None]), 0.0)
        factor = jnp.exp(running - raised)
        denominator = denominator * factor + jnp.sum(block_probs, axis=-1)
        weighted = weighted * factor[..., None] + jnp.einsum(
            "hqk,khd->hqd",
            block_probs.astype(jnp.bfloat16),
            value_heads,
            preferred_element_type=jnp.float32,
        )
        return ((raised, denominator, weighted), None)

    state, _ = lax.scan(
        fold_inner, initial, (key_blocks, value_blocks, jnp.arange(count, dtype=jnp.int32))
    )
    running, denominator, weighted = state
    attended = (weighted / denominator[..., None]).transpose(1, 0, 2).reshape(rows, width)
    log_total = running + jnp.log(denominator)
    attended_low = attended.astype(jnp.bfloat16)
    branch = jnp.dot(attended_low, w_out, preferred_element_type=jnp.float32) + b_out
    first_sum = inputs.astype(jnp.float32) + branch
    normed = layer_norm(first_sum, gain[0], shift[0]).astype(jnp.bfloat16)
    up_pre = jnp.dot(normed, w_up, preferred_element_type=jnp.float32) + b_up
    activated = exact_gelu(up_pre).astype(jnp.bfloat16)
    second_sum = (
        normed.astype(jnp.float32)
        + jnp.dot(activated, w_down, preferred_element_type=jnp.float32)
        + b_down
    )
    output = layer_norm(second_sum, gain[1], shift[1])
    kept = (
        inputs,
        queries,
        keys,
        values,
        attended,
        attended_low,
        log_total,
        None,
        first_sum,
        normed,
        up_pre,
        activated,
        second_sum,
    )
    return (output, kept)


def attention_grads(kept, grad_att, query_seg, lengths, valid):
    (
        inputs,
        queries,
        keys,
        values,
        attended,
        attended_low,
        log_total,
        gathered,
        first_sum,
        normed,
        up_pre,
        activated,
        second_sum,
    ) = kept
    rows, width = queries.shape
    scale = (width // HEADS) ** (-0.5)
    query_heads = split_heads(queries)
    grad_heads = split_heads(grad_att)
    correction = jnp.sum(grad_heads.astype(jnp.float32) * split_heads(attended), axis=-1).T
    key_all, value_all = (
        lax.all_gather(keys, "seq", axis=0, tiled=True),
        lax.all_gather(values, "seq", axis=0, tiled=True),
    )
    count = key_all.shape[0] // rows
    key_blocks = key_all.reshape(count, rows, HEADS, -1)
    value_blocks = value_all.reshape(count, rows, HEADS, -1)
    block_ids = jnp.arange(count, dtype=jnp.int32)
    zero_heads = jnp.zeros((rows, HEADS, width // HEADS), jnp.float32)

    def attention_inner(acc, item):
        key_heads, value_heads, block_at = item
        _, block_tag = clip_tags(lengths, valid, block_at * rows, rows)
        probs, grad_scores = pair_terms(
            query_heads,
            grad_heads,
            log_total,
            correction,
            query_seg,
            key_heads,
            value_heads,
            block_tag,
            scale,
        )
        acc = (
            acc
            + jnp.einsum("hqk,khd->qhd", grad_scores, key_heads, preferred_element_type=jnp.float32)
            * scale
        )
        key_term = (
            jnp.einsum("hqk,qhd->khd", grad_scores, query_heads, preferred_element_type=jnp.float32)
            * scale
        )
        value_term = jnp.einsum(
            "hqk,qhd->khd", probs, grad_heads, preferred_element_type=jnp.float32
        )
        return (
            acc,
            jnp.concatenate(
                [key_term.reshape(rows, width), value_term.reshape(rows, width)], axis=1
            ),
        )

    grad_query, terms = lax.scan(attention_inner, zero_heads, (key_blocks, value_blocks, block_ids))
    summed = lax.psum_scatter(
        terms.reshape(count * rows, 2 * width).astype(jnp.bfloat16),
        "seq",
        scatter_dimension=0,
        tiled=True,
    ).astype(jnp.float32)
    grad_key = summed[:, :width]
    grad_value = summed[:, width:]
    return (grad_query.reshape(rows, width), grad_key, grad_value)


def backward_layer(grad_out, kept, weights, query_seg, lengths, valid):
    w_qkv, b_qv, w_out, b_out, gain, shift, w_up, b_up, w_down, b_down = weights
    (
        inputs,
        queries,
        keys,
        values,
        attended,
        attended_low,
        log_total,
        gathered,
        first_sum,
        normed,
        up_pre,
        activated,
        second_sum,
    ) = kept
    _, pull_second = jax.vjp(layer_norm, second_sum, gain[1], shift[1])
    grad_second, gain_second, shift_second = pull_second(grad_out)
    grad_down = grad_second.astype(jnp.bfloat16)
    sum_down = jnp.sum(grad_down, axis=0, dtype=jnp.float32)
    weight_down = jnp.einsum("rf,rd->fd", activated, grad_down, preferred_element_type=jnp.float32)
    grad_activated = jnp.einsum("rd,fd->rf", grad_down, w_down, preferred_element_type=jnp.float32)
    _, pull_gelu = jax.vjp(exact_gelu, up_pre)
    grad_up = pull_gelu(grad_activated)[0].astype(jnp.bfloat16)
    sum_up = jnp.sum(grad_up, axis=0, dtype=jnp.float32)
    weight_up = jnp.einsum("rd,rf->df", normed, grad_up, preferred_element_type=jnp.float32)
    grad_normed = grad_second + jnp.einsum(
        "rf,df->rd", grad_up, w_up, preferred_element_type=jnp.float32
    )
    _, pull_first = jax.vjp(layer_norm, first_sum, gain[0], shift[0])
    grad_first, gain_first, shift_first = pull_first(grad_normed)
    grad_branch = grad_first.astype(jnp.bfloat16)
    sum_out = jnp.sum(grad_branch, axis=0, dtype=jnp.float32)
    weight_out = jnp.einsum(
        "re,rd->ed", attended_low, grad_branch, preferred_element_type=jnp.float32
    )
    grad_att = jnp.einsum(
        "rd,ed->re", grad_branch, w_out, preferred_element_type=jnp.float32
    ).astype(jnp.bfloat16)
    grad_query, grad_key, grad_value = attention_grads(kept, grad_att, query_seg, lengths, valid)
    grad_proj = jnp.concatenate(
        [
            grad_query.astype(jnp.bfloat16),
            grad_key.astype(jnp.bfloat16),
            grad_value.astype(jnp.bfloat16),
        ],
        axis=1,
    )
    width = inputs.shape[1]
    sum_qv = jnp.concatenate(
        [
            jnp.sum(grad_proj[:, :width], axis=0, dtype=jnp.float32),
            jnp.sum(grad_proj[:, 2 * width :], axis=0, dtype=jnp.float32),
        ]
    )
    weight_qkv = jnp.einsum("rd,re->de", inputs, grad_proj, preferred_element_type=jnp.float32)
    grad_input = grad_first + jnp.einsum(
        "re,de->rd", grad_proj, w_qkv, preferred_element_type=jnp.float32
    )
    gains = jnp.stack([gain_first, gain_second])
    shifts = jnp.stack([shift_first, shift_second])
    return (
        grad_input,
        (
            weight_qkv,
            sum_qv,
            weight_out,
            sum_out,
            gains,
            shifts,
            weight_up,
            sum_up,
            weight_down,
            sum_down,
        ),
    )


def local(
    frames,
    w_qkv,
    b_qv,
    w_out,
    b_out,
    ln_gain,
    ln_shift,
    w_up,
    b_up,
    w_down,
    b_down,
    cotangent,
    clip_lengths,
    valid_lengths,
):
    rows = frames.shape[1]
    lengths = clip_lengths[0]
    valid = valid_lengths[0]
    offset = lax.axis_index("seq") * rows
    query_seg, key_tag = clip_tags(lengths, valid, offset, rows)
    layer_weights = [
        tuple(
            (
                array[layer_at]
                for array in (
                    w_qkv,
                    b_qv,
                    w_out,
                    b_out,
                    ln_gain,
                    ln_shift,
                    w_up,
                    b_up,
                    w_down,
                    b_down,
                )
            )
        )
        for layer_at in range(LAYERS)
    ]
    hidden = frames[0].astype(jnp.float32)
    saved = []
    for layer_at in range(LAYERS):
        hidden, kept = forward_layer(hidden, layer_weights[layer_at], query_seg, lengths, valid)
        saved.append(kept)
    activations = hidden.astype(jnp.bfloat16)[None]
    grad_hidden = cotangent[0].astype(jnp.float32)
    per_layer = [None] * LAYERS
    for layer_at in reversed(range(LAYERS)):
        grad_hidden, per_layer[layer_at] = backward_layer(
            grad_hidden, saved[layer_at], layer_weights[layer_at], query_seg, lengths, valid
        )
    stacked = [
        jnp.stack([per_layer[layer_at][member] for layer_at in range(LAYERS)])
        for member in range(10)
    ]
    g_wqkv, g_bqv, g_wout, g_bout, g_gain, g_shift, g_wup, g_bup, g_wdown, g_bdown = stacked
    shares = (
        lax.psum_scatter(
            g_wqkv.astype(jnp.bfloat16), "seq", scatter_dimension=1, tiled=True
        ).astype(jnp.float32),
        lax.psum_scatter(g_bqv.astype(jnp.bfloat16), "seq", scatter_dimension=1, tiled=True).astype(
            jnp.float32
        ),
        lax.psum_scatter(
            g_wout.astype(jnp.bfloat16), "seq", scatter_dimension=1, tiled=True
        ).astype(jnp.float32),
        lax.psum_scatter(
            g_bout.astype(jnp.bfloat16), "seq", scatter_dimension=1, tiled=True
        ).astype(jnp.float32),
        lax.psum_scatter(
            g_gain.astype(jnp.bfloat16), "seq", scatter_dimension=2, tiled=True
        ).astype(jnp.float32),
        lax.psum_scatter(
            g_shift.astype(jnp.bfloat16), "seq", scatter_dimension=2, tiled=True
        ).astype(jnp.float32),
        lax.psum_scatter(g_wup.astype(jnp.bfloat16), "seq", scatter_dimension=1, tiled=True).astype(
            jnp.float32
        ),
        lax.psum_scatter(g_bup.astype(jnp.bfloat16), "seq", scatter_dimension=1, tiled=True).astype(
            jnp.float32
        ),
        lax.psum_scatter(
            g_wdown.astype(jnp.bfloat16), "seq", scatter_dimension=1, tiled=True
        ).astype(jnp.float32),
        lax.psum_scatter(
            g_bdown.astype(jnp.bfloat16), "seq", scatter_dimension=1, tiled=True
        ).astype(jnp.float32),
    )
    s_wqkv, s_bqv, s_wout, s_bout, s_gain, s_shift, s_wup, s_bup, s_wdown, s_bdown = shares
    totals = (
        lax.psum(s_wqkv.astype(jnp.bfloat16), "bucket").astype(jnp.float32),
        lax.psum(s_bqv.astype(jnp.bfloat16), "bucket").astype(jnp.float32),
        lax.psum(s_wout.astype(jnp.bfloat16), "bucket").astype(jnp.float32),
        lax.psum(s_bout.astype(jnp.bfloat16), "bucket").astype(jnp.float32),
        lax.psum(s_gain.astype(jnp.bfloat16), "bucket").astype(jnp.float32),
        lax.psum(s_shift.astype(jnp.bfloat16), "bucket").astype(jnp.float32),
        lax.psum(s_wup.astype(jnp.bfloat16), "bucket").astype(jnp.float32),
        lax.psum(s_bup.astype(jnp.bfloat16), "bucket").astype(jnp.float32),
        lax.psum(s_wdown.astype(jnp.bfloat16), "bucket").astype(jnp.float32),
        lax.psum(s_bdown.astype(jnp.bfloat16), "bucket").astype(jnp.float32),
    )
    return (
        activations,
        grad_hidden[None],
        totals[0],
        totals[1],
        totals[2],
        totals[3],
        totals[4],
        totals[5],
        totals[6],
        totals[7],
        totals[8],
        totals[9],
    )


def solution(mesh):
    placed = (
        P("bucket", "seq", None),
        P(),
        P(),
        P(),
        P(),
        P(),
        P(),
        P(),
        P(),
        P(),
        P(),
        P("bucket", "seq", None),
        P("bucket", None),
        P("bucket", None),
    )
    return jax.shard_map(
        local,
        mesh=mesh,
        in_specs=placed,
        out_specs=(
            P("bucket", "seq", None),
            P("bucket", "seq", None),
            P(None, "seq", None),
            P(None, "seq"),
            P(None, "seq", None),
            P(None, "seq"),
            P(None, None, "seq"),
            P(None, None, "seq"),
            P(None, "seq", None),
            P(None, "seq"),
            P(None, "seq", None),
            P(None, "seq"),
        ),
        check_vma=False,
    )
```

profile of v0, /device:TPU:0, one launch (start us, length us, event | category | flops | bytes accessed | tf_op | source)
XLA Modules:
  0.0 1489.1 jit_solution(11088479508015124055)
XLA Ops:
  8.6 3.2 fusion.128
  19.6 28.4 %all-gather.7.cloned.1.call-done = bf16[2048,768]{1,0:T(8,128)(2,1)} async-done(((bf16[256,768]{1,0:T(8,128)(2,1)}), bf16[2048,768]{1,0:T(8,128)(2,1)}) %all-gather.7.cloned.1.call-update) | async-done | bytes 3145744 | tf_op jit(solution)/shard_map/all_gather | solution.py:76
  48.0 3.2 copy.155
  52.3 2.4 copy.157
  54.7 28.1 %all-gather.5.cloned.1.call-done = bf16[2048,768]{1,0:T(8,128)(2,1)} async-done(((bf16[256,768]{1,0:T(8,128)(2,1)}), bf16[2048,768]{1,0:T(8,128)(2,1)}) %all-gather.5.cloned.1.call-update) | async-done | bytes 3145744 | tf_op jit(solution)/shard_map/all_gather | solution.py:75
  82.8 3.2 copy.153
  90.0 99.3 %while.68 = (s32[]{:T(128)}, f32[12,256]{1,0:T(8,128)S(1)}, f32[12,256]{1,0:T(8,128)}, f32[12,256,64]{1,2,0:T(8,128)}, s32[256]{0:T(256)}, /*index=5*/s32[8]{0:T...) while((s32[]{:T(128)}, f32[12,256]{1,0:T(8,128)S(1)}, ...), condition=%wide.region_7.8_spmd.clone, body=%wide.region_2.7_spmd.clone.sunk | while | flops 212243456 | bytes 19572732 | solution.py:103
  193.2 12.3 multiply_convert_fusion.1
  210.7 31.4 %all-gather.11.cloned.1.call-done = bf16[2048,768]{1,0:T(8,128)(2,1)} async-done(((bf16[256,768]{1,0:T(8,128)(2,1)}), bf16[2048,768]{1,0:T(8,128)(2,1)}) %all-gather.11.cloned.1.call-update) | async-done | bytes 3145744 | tf_op jit(solution)/shard_map/all_gather | solution.py:76
  242.0 3.2 copy.160
  246.3 2.4 copy.162
  248.7 27.9 %all-gather.9.cloned.1.call-done = bf16[2048,768]{1,0:T(8,128)(2,1)} async-done(((bf16[256,768]{1,0:T(8,128)(2,1)}), bf16[2048,768]{1,0:T(8,128)(2,1)}) %all-gather.9.cloned.1.call-update) | async-done | bytes 3145744 | tf_op jit(solution)/shard_map/all_gather | solution.py:75
  276.7 3.2 copy.158
  281.0 2.4 copy.161
  283.9 104.3 %while.69 = (s32[]{:T(128)}, f32[12,256]{1,0:T(8,128)}, f32[12,256]{1,0:T(8,128)}, f32[12,256,64]{1,2,0:T(8,128)}, s32[256]{0:T(256)}, /*index=5*/s32[8]{0:T(128...) while((s32[]{:T(128)}, f32[12,256]{1,0:T(8,128)}, ...), condition=%wide.region_17.18_spmd.clone, body=%wide.region_12.17_spmd.clone.sunk | while | flops 212243456 | bytes 19621912 | solution.py:103
  392.1 10.1 multiply_convert_fusion
  407.0 3.0 fusion.228
  415.3 3.2 broadcast.505.clone2
  418.5 103.7 %while.70 = (s32[]{:T(128)}, f32[256,12,64]{0,2,1:T(8,128)}, bf16[8,256,1536]{2,1,0:T(8,128)(2,1)}, bf16[8,256,12,64]{1,3,2,0:T(8,128)(2,1)}, s32[256]{0:T(256)}...) while((s32[]{:T(128)}, f32[256,12,64]{0,2,1:T(8,128)}, ...), condition=%wide.region_30.31_spmd.clone, body=%wide.region_27.30_spmd.clone.sunk | while | flops 515397632 | bytes 27573572 | solution.py:203
  441.6 2.6 fusion.332
  454.6 2.6 fusion.332
  467.6 2.6 fusion.332
  480.6 2.6 fusion.332
  493.6 2.6 fusion.332
  506.6 2.6 fusion.332
  519.6 2.6 fusion.332
  524.3 59.9 %reduce-scatter.24.cloned.1.call-done = bf16[256,1536]{1,0:T(8,128)(2,1)} async-done(((bf16[2048,1536]{1,0:T(8,128)(2,1)}), bf16[256,1536]{1,0:T(8,128)(2,1)}) %reduce-scatter.24.cloned.1.call-update) | async-done | bytes 786448 | tf_op jit(solution)/shard_map/reduce_scatter | solution.py:204
  584.3 4.3 multiply_reduce_fusion.1
  590.5 5.5 fusion.229
  601.9 3.2 broadcast.505.clone
  605.1 102.6 %while.71 = (s32[]{:T(128)}, f32[256,12,64]{0,2,1:T(8,128)}, bf16[8,256,1536]{2,1,0:T(8,128)(2,1)}, bf16[8,256,12,64]{1,3,2,0:T(8,128)(2,1)}, s32[256]{0:T(256)}...) while((s32[]{:T(128)}, f32[256,12,64]{0,2,1:T(8,128)}, ...), condition=%wide.region_40.41_spmd.clone, body=%wide.region_37.40_spmd.clone.sunk | while | flops 515397632 | bytes 27573260 | solution.py:203
  628.0 2.6 fusion.346
  640.8 2.6 fusion.346
  653.7 2.6 fusion.346
  666.6 2.6 fusion.346
  679.4 2.6 fusion.346
  692.3 2.6 fusion.346
  705.1 2.6 fusion.346
  710.5 2.7 fusion.103
  713.3 56.4 %reduce-scatter.26.cloned.1.call-done = bf16[256,1536]{1,0:T(8,128)(2,1)} async-done(((bf16[2048,1536]{1,0:T(8,128)(2,1)}), bf16[256,1536]{1,0:T(8,128)(2,1)}) %reduce-scatter.26.cloned.1.call-update) | async-done | bytes 786448 | tf_op jit(solution)/shard_map/reduce_scatter | solution.py:204
  769.6 2.5 fusion.102
  772.1 3.5 pad_maximum_fusion.2
  775.6 18.2 %copy.174 = bf16[2,768,2304]{2,0,1:T(2,128)(2,1)} copy(bf16[2,768,2304]{1,2,0:T(8,128)(2,1)} %pad_maximum_fusion.2) | data formatting | bytes 14155776 | tf_op jit(solution)/shard_map/stack | solution.py:348
  798.2 3.7 fusion.107
  801.9 3.6 fusion.106
  805.5 8.5 pad_maximum_fusion.1
  815.7 3.8 fusion.105
  819.6 3.7 fusion.104
  823.3 8.4 pad_maximum_fusion
  841.9 65.0 %all-reduce.6.cloned.1.call-done = bf16[2,768,2304]{2,0,1:T(2,128)(2,1)} async-done(((bf16[2,768,2304]{2,0,1:T(2,128)(2,1)}), bf16[2,768,2304]{2,0,1:T(2,128)(2,1)}) %all-reduce.6.cloned.1.call-update) | async-done | bytes 7077904
  906.9 2.7 constant_dynamic-slice_fusion
  909.6 43.9 %reduce-scatter.28.cloned.1.call-done = bf16[2,96,768]{2,1,0:T(8,128)(2,1)} async-done(((bf16[2,768,768]{2,1,0:T(8,128)(2,1)}), bf16[2,96,768]{2,1,0:T(8,128)(2,1)}) %reduce-scatter.28.cloned.1.call-update) | async-done | bytes 294928 | tf_op jit(solution)/shard_map/reduce_scatter | solution.py:359
  953.5 80.4 %reduce-scatter.32.cloned.1.call-done = bf16[2,384,768]{2,1,0:T(8,128)(2,1)} async-done(((bf16[2,3072,768]{2,1,0:T(8,128)(2,1)}), bf16[2,384,768]{2,1,0:T(8,128)(2,1)}) %reduce-scatter.32.cloned.1.call-update) | async-done | bytes 1179664 | tf_op jit(solution)/shard_map/reduce_scatter | solution.py:377
  1033.9 80.3 %reduce-scatter.30.cloned.1.call-done = bf16[2,96,3072]{2,1,0:T(8,128)(2,1)} async-done(((bf16[2,768,3072]{2,1,0:T(8,128)(2,1)}), bf16[2,96,3072]{2,1,0:T(8,128)(2,1)}) %reduce-scatter.30.cloned.1.call-update) | async-done | bytes 1179664 | tf_op jit(solution)/shard_map/reduce_scatter | solution.py:371
  1114.2 36.9 %reduce-scatter.44.cloned.1.call-done = bf16[96,2]{1,0:T(8,128)(2,1)} async-done(((bf16[768,2]{1,0:T(8,128)(2,1)}), bf16[96,2]{1,0:T(8,128)(2,1)}) %reduce-scatter.44.cloned.1.call-update) | async-done | bytes 400
  1151.9 35.6 %reduce-scatter.36.cloned.1.call-done = bf16[96,2]{1,0:T(8,128)(2,1)} async-done(((bf16[768,2]{1,0:T(8,128)(2,1)}), bf16[96,2]{1,0:T(8,128)(2,1)}) %reduce-scatter.36.cloned.1.call-update) | async-done | bytes 400
  1188.3 36.1 %reduce-scatter.40.cloned.1.call-done = bf16[96,4]{1,0:T(8,128)(2,1)} async-done(((bf16[768,4]{1,0:T(8,128)(2,1)}), bf16[96,4]{1,0:T(8,128)(2,1)}) %reduce-scatter.40.cloned.1.call-update) | async-done | bytes 784
  1225.4 35.5 %reduce-scatter.38.cloned.1.call-done = bf16[96,4]{1,0:T(8,128)(2,1)} async-done(((bf16[768,4]{1,0:T(8,128)(2,1)}), bf16[96,4]{1,0:T(8,128)(2,1)}) %reduce-scatter.38.cloned.1.call-update) | async-done | bytes 784
  1261.8 38.0 %reduce-scatter.42.cloned.1.call-done = bf16[384,2]{1,0:T(8,128)(2,1)} async-done(((bf16[3072,2]{1,0:T(8,128)(2,1)}), bf16[384,2]{1,0:T(8,128)(2,1)}) %reduce-scatter.42.cloned.1.call-update) | async-done | bytes 1552
  1300.8 4.0 fusion.157
  1304.8 32.6 %reduce-scatter.34.cloned.1.call-done = bf16[192,2]{1,0:T(8,128)(2,1)} async-done(((bf16[1536,2]{1,0:T(8,128)(2,1)}), bf16[192,2]{1,0:T(8,128)(2,1)}) %reduce-scatter.34.cloned.1.call-update) | async-done | bytes 784
  1338.3 12.0 all-reduce.1
  1353.7 121.8 %all-reduce.8.cloned.1.call-done = (bf16[2,96,2304]{2,0,1:T(2,128)(2,1)}, bf16[2,96,768]{2,1,0:T(8,128)(2,1)}, bf16[2,96,3072]{2,1,0:T(8,128)(2,1)}, bf16[2,384,768]{2,1,0:T(8,128)(2,1)}) async-done(((bf16[2,96,2304]{2,0,1:T(2,128)(2,1)}, bf16[2,96,768]{2,1,0:T(8,128)(2,1)}, bf16[2,96,3072]{2,1,0:T(8,128)(2,1)}, bf16[2,384,768]{2,1,0:T(8,128)(2,1)}), (bf16[2,96,2304]{2,0,1:T(2,128)(2,1)}, ...) | async-done | bytes 3538960 | tf_op jit(solution)/shard_map/psum | solution.py:386
  1475.5 3.1 convert_element_type.306
  (1285 shorter events, 428.2 us)
Async XLA Ops:
  7.2 40.8 %all-gather.7.cloned.1.call-start = ((), (), s32[]{:S(2)}) async-start(), calls=%async_computation.12 | async-start | bytes 3538944 | tf_op jit(solution)/shard_map/all_gather | solution.py:76
  12.8 70.0 %all-gather.5.cloned.1.call-start = ((), (), s32[]{:S(2)}) async-start(), calls=%async_computation.11 | async-start | bytes 3538944 | tf_op jit(solution)/shard_map/all_gather | solution.py:75
  13.7 228.3 %all-gather.11.cloned.1.call-start = ((), (), s32[]{:S(2)}) async-start(), calls=%async_computation.14 | async-start | bytes 3538944 | tf_op jit(solution)/shard_map/all_gather | solution.py:76
  189.3 16.2 %copy-start = (bf16[256,12,64]{0,2,1:T(8,128)(2,1)}, bf16[256,12,64]{0,2,1:T(8,128)(2,1)S(1)}, u32[]{:S(2)}) copy-start(bf16[256,12,64]{0,2,1:T(8,128)(2,1)S(1)} %get-tuple-element.1983) | copy-start | bytes 1179652
  190.7 14.8 copy-start.47
  190.7 14.9 slice-start
  190.7 16.7 %slice-start.12 = ((s8[7077888]{0:T(1024)(128)(4,1)}), s8[4194304]{0:T(1024)(128)(4,1)S(1)}, s32[]{:S(2)}) async-start(s8[7077888]{0:T(1024)(128)(4,1)} %bitcast.530), calls=%async_computation.40 | async-start | bytes 8388608
  192.8 12.7 copy-start.8
  192.8 12.7 copy-start.83
  193.1 12.4 copy-start.113
  193.1 12.4 copy-start.95
  193.1 12.4 copy-start.127
  193.1 12.4 slice-start.1
  193.1 12.4 slice-start.2
  193.2 14.2 slice-start.13
  209.5 67.1 %all-gather.9.cloned.1.call-start = ((), (), s32[]{:S(2)}) async-start(), calls=%async_computation.13 | async-start | bytes 3538944 | tf_op jit(solution)/shard_map/all_gather | solution.py:75
  210.4 373.8 %reduce-scatter.24.cloned.1.call-start = ((), (), s32[]{:S(2)}) async-start(), calls=%async_computation.15 | async-start | bytes 7077888 | tf_op jit(solution)/shard_map/reduce_scatter | solution.py:204
  389.5 12.8 copy-start.49
  389.5 12.8 slice-start.3
  391.8 20.6 %copy-start.13 = (f32[256,768]{1,0:T(8,128)}, f32[256,768]{1,0:T(8,128)S(1)}, u32[]{:S(2)}) copy-start(f32[256,768]{1,0:T(8,128)S(1)} %get-tuple-element.1420) | copy-start | bytes 2359300
  391.8 20.6 %copy-start.86 = (f32[256]{0:T(256)}, f32[256]{0:T(256)S(1)}, u32[]{:S(2)}) copy-start(f32[256]{0:T(256)S(1)} %broadcast_multiply_fusion.1) | copy-start | bytes 3076
  392.1 20.3 %copy-start.98 = (f32[256]{0:T(256)}, f32[256]{0:T(256)S(1)}, u32[]{:S(2)}) copy-start(f32[256]{0:T(256)S(1)} %fusion.204) | copy-start | bytes 3076
  392.1 10.2 copy-start.126
  392.1 10.2 slice-start.4
  392.1 10.2 slice-start.5
  418.5 8.2 copy-start.41
  418.5 8.2 copy-start.107
  431.2 8.2 copy-start.41
  431.2 8.2 copy-start.107
  444.3 8.2 copy-start.41
  457.2 8.2 copy-start.41
  457.3 8.2 copy-start.107
  470.2 8.2 copy-start.41
  470.3 8.2 copy-start.107
  483.2 8.2 copy-start.41
  496.2 8.2 copy-start.41
  509.2 8.2 copy-start.41
  509.2 8.2 copy-start.107
  522.2 62.0 %copy-start.12 = (f32[256,768]{1,0:T(8,128)S(1)}, f32[256,768]{1,0:T(8,128)}, u32[]{:S(2)}) copy-start(f32[256,768]{1,0:T(8,128)} %copy-done.11) | copy-start | bytes 2359300
  522.2 62.0 %copy-start.30 = (f32[256,768]{1,0:T(8,128)S(1)}, f32[256,768]{1,0:T(8,128)}, u32[]{:S(2)}) copy-start(f32[256,768]{1,0:T(8,128)} %copy-done.29) | copy-start | bytes 2359300
  522.2 62.0 %copy-start.71 = (f32[768]{0:T(1024)S(1)}, f32[768]{0:T(1024)}, u32[]{:S(2)}) copy-start(f32[768]{0:T(1024)} %get-tuple-element.1433) | copy-start | bytes 9220
  522.2 62.0 %copy-start.81 = (f32[256]{0:T(256)S(1)}, f32[256]{0:T(256)}, u32[]{:S(2)}) copy-start(f32[256]{0:T(256)} %copy-done.80) | copy-start | bytes 3076
  522.2 62.0 %copy-start.90 = (f32[256]{0:T(256)S(1)}, f32[256]{0:T(256)}, u32[]{:S(2)}) copy-start(f32[256]{0:T(256)} %copy-done.89) | copy-start | bytes 3076
  522.2 62.0 %copy-start.131 = (f32[256]{0:T(256)S(1)}, f32[256]{0:T(256)}, u32[]{:S(2)}) copy-start(f32[256]{0:T(256)} %copy-done.130) | copy-start | bytes 3076
  522.3 247.4 %reduce-scatter.26.cloned.1.call-start = ((), (), s32[]{:S(2)}) async-start(), calls=%async_computation.16 | async-start | bytes 7077888 | tf_op jit(solution)/shard_map/reduce_scatter | solution.py:204
  524.3 64.3 %copy-start.38 = (bf16[256,768]{1,0:T(8,128)(2,1)}, bf16[256,768]{1,0:T(8,128)(2,1)S(1)}, u32[]{:S(2)}) copy-start(bf16[256,768]{1,0:T(8,128)(2,1)S(1)} %copy.167) | copy-start | bytes 1179652
  524.3 64.3 %copy-start.116 = (f32[256]{0:T(256)S(1)}, f32[256]{0:T(256)}, u32[]{:S(2)}) copy-start(f32[256]{0:T(256)} %copy-done.115) | copy-start | bytes 3076
  584.2 11.7 slice-start.9
  707.8 199.1 %all-reduce.6.cloned.1.call-start = ((), (), s32[]{:S(2)}) async-start(), calls=%async_computation.26 | async-start | bytes 14155776
  793.9 159.6 %reduce-scatter.28.cloned.1.call-start = ((), (), s32[]{:S(2)}) async-start(), calls=%async_computation.17 | async-start | bytes 2654208 | tf_op jit(solution)/shard_map/reduce_scatter | solution.py:359
  797.6 236.3 %reduce-scatter.32.cloned.1.call-start = ((), (), s32[]{:S(2)}) async-start(), calls=%async_computation.19 | async-start | bytes 10616832 | tf_op jit(solution)/shard_map/reduce_scatter | solution.py:377
  814.1 300.1 %reduce-scatter.30.cloned.1.call-start = ((), (), s32[]{:S(2)}) async-start(), calls=%async_computation.18 | async-start | bytes 10616832 | tf_op jit(solution)/shard_map/reduce_scatter | solution.py:371
  831.9 8.7 copy-start.104
  831.9 8.8 copy-start.65
  831.9 319.2 %reduce-scatter.44.cloned.1.call-start = ((), (), s32[]{:S(2)}) async-start(), calls=%async_computation.25 | async-start | bytes 221184
  835.3 352.2 %reduce-scatter.36.cloned.1.call-start = ((), (), s32[]{:S(2)}) async-start(), calls=%async_computation.21 | async-start | bytes 221184
  836.3 388.1 %reduce-scatter.40.cloned.1.call-start = ((), (), s32[]{:S(2)}) async-start(), calls=%async_computation.23 | async-start | bytes 221184
  837.7 423.1 %reduce-scatter.38.cloned.1.call-start = ((), (), s32[]{:S(2)}) async-start(), calls=%async_computation.22 | async-start | bytes 221184
  839.2 460.6 %reduce-scatter.42.cloned.1.call-start = ((), (), s32[]{:S(2)}) async-start(), calls=%async_computation.24 | async-start | bytes 884736
  840.7 496.7 %reduce-scatter.34.cloned.1.call-start = ((), (), s32[]{:S(2)}) async-start(), calls=%async_computation.20 | async-start | bytes 442368
  841.8 458.9 %copy-start.28 = (f32[256,768]{1,0:T(8,128)S(1)}, f32[256,768]{1,0:T(8,128)}, u32[]{:S(2)}) copy-start(f32[256,768]{1,0:T(8,128)} %copy-done.27) | copy-start | bytes 2359300
  841.8 458.9 %copy-start.63 = (bf16[256,768]{1,0:T(8,128)(2,1)S(1)}, bf16[256,768]{1,0:T(8,128)(2,1)}, u32[]{:S(2)}) copy-start(bf16[256,768]{1,0:T(8,128)(2,1)} %copy.172) | copy-start | bytes 1179652
  841.8 458.9 %copy-start.129 = (f32[256]{0:T(256)S(1)}, f32[256]{0:T(256)}, u32[]{:S(2)}) copy-start(f32[256]{0:T(256)} %copy-done.128) | copy-start | bytes 3076
  841.9 633.6 %all-reduce.8.cloned.1.call-start = ((), (), s32[]{:S(2)}) async-start(), calls=%async_computation.27 | async-start | bytes 7077888 | tf_op jit(solution)/shard_map/psum | solution.py:386
  (303 other events, 958.8 us)
Sparse Core Ops, SparseCore 0:
  12.9 35.0 all-gather.6
  50.4 32.3 all-gather.4
  209.7 32.3 all-gather.10
  244.3 32.3 all-gather.8
  522.4 61.7 reduce-scatter.23
  707.9 61.7 reduce-scatter.25
  794.0 112.8 all-reduce.5
  910.8 42.5 reduce-scatter.27
  957.4 76.4 reduce-scatter.31
  1037.6 76.4 reduce-scatter.29
  1117.5 33.5 reduce-scatter.43
  1154.0 33.5 reduce-scatter.35
  1190.8 33.5 reduce-scatter.39
  1227.3 33.5 reduce-scatter.37
  1264.8 34.9 reduce-scatter.41
  1303.5 33.8 reduce-scatter.33
  1340.6 134.8 all-reduce.7
where the time goes:
time: 1510 us; the launch traced here: 1490 us
  waiting for transfers between devices  838 us (55%)
  matrix products  270 us (18%)
  local copies, waits for them, and re-layouts  165 us (11%)
  other arithmetic  160 us (11%)
  loops' own time  24.7 us (2%)
  between operations  16.9 us (1%)
    unnamed x24, waiting for transfers between devices  280 us
    psum x1, waiting for transfers between devices, local(): lax.psum(s_wqkv.astype(jnp.bfloat16), 'bucket').astype(jnp.float32)  122 us
    reduce_scatter x2, waiting for transfers between devices, attention_grads(): lax.psum_scatter(terms.reshape(count * rows, 2 * width).astype(jnp.bfloat...  116 us
    reduce_scatter x1, waiting for transfers between devices, local(): lax.psum_scatter(g_wdown.astype(jnp.bfloat16), 'seq', scatter_dimension=1...  80.4 us
    reduce_scatter x1, waiting for transfers between devices, local(): lax.psum_scatter(g_wup.astype(jnp.bfloat16), 'seq', scatter_dimension=1,...  80.3 us
    all_gather x2, waiting for transfers between devices, forward_layer(): value_piece = lax.all_gather(values, 'seq', axis=0, tiled=True)  59.7 us
    all_gather x2, waiting for transfers between devices, forward_layer(): key_piece = lax.all_gather(keys, 'seq', axis=0, tiled=True)  56 us
    reduce_scatter x1, waiting for transfers between devices, local(): lax.psum_scatter(g_wout.astype(jnp.bfloat16), 'seq', scatter_dimension=1,...  43.9 us
  transfers between devices with their start and end apart: 17, of which 17 were waited for; matrix products, arithmetic and copies ran while one was open for 6% of the time, Pallas kernels for 0%

commit v1 on v0

--- a/solution.py
+++ b/solution.py
@@ -1,10 +1,810 @@
+import functools
+import math
+
 import jax
 import jax.numpy as jnp
 from jax import lax
+from jax.experimental import pallas as pl
+from jax.experimental.pallas import tpu as pltpu
 from jax.sharding import PartitionSpec as P
 
 HEADS = 12
 LAYERS = 2
+BF = jnp.bfloat16
+F32 = jnp.float32
+LOW = -1e30
+SLACK = 8 * 1024 * 1024
+
+
+def dot_nn(a, b):
+    return lax.dot_general(a, b, (((1,), (0,)), ((), ())), preferred_element_type=F32)
+
+
+def dot_nt(a, b):
+    return lax.dot_general(a, b, (((1,), (1,)), ((), ())), preferred_element_type=F32)
+
+
+def block_bytes(spec, array):
+    lanes = [n for n in spec.block_shape if n is not None]
+    lanes[-1] += -lanes[-1] % 128
+    return math.prod(lanes) * array.dtype.itemsize
+
+
+def call(body, name, out_shape, in_specs, out_specs, grid, scratch, flops, args, scalars):
+    out_bytes = sum(s.size * s.dtype.itemsize for s in jax.tree.leaves(out_shape))
+    need = sum(block_bytes(p, a) for p, a in zip(in_specs, args))
+    need += sum(block_bytes(p, a) for p, a in zip(jax.tree.leaves(out_specs), jax.tree.leaves(out_shape)))
+    need = 2 * need + sum(math.prod(m.shape) * jnp.dtype(m.dtype).itemsize for m in scratch)
+    return pl.pallas_call(
+        body,
+        name=name,
+        out_shape=out_shape,
+        grid_spec=pltpu.PrefetchScalarGridSpec(
+            num_scalar_prefetch=1,
+            grid=grid,
+            in_specs=in_specs,
+            out_specs=out_specs,
+            scratch_shapes=scratch,
+        ),
+        compiler_params=pltpu.CompilerParams(vmem_limit_bytes=need + SLACK),
+        cost_estimate=pl.CostEstimate(
+            flops=int(flops), bytes_accessed=int(out_bytes * 3), transcendentals=0
+        ),
+    )(scalars, *args)
+
+
+def whole(shape):
+    return pl.BlockSpec(shape, lambda i, s: (0,) * len(shape))
+
+
+def sds(shape, dtype=BF):
+    return jax.ShapeDtypeStruct(shape, dtype)
+
+
+def attend_kernel(layer, chips, first, last, *refs):
+    refs = list(refs)
+    refs.pop(0)
+    if not first:
+        qt_in, acc_in, m_in = refs.pop(0), refs.pop(0), refs.pop(0)
+    seg_ref, bias_ref, wk_ref, wv_ref = (refs.pop(0) for _ in range(4))
+    if first:
+        wq_ref = refs.pop(0)
+    bias_k = refs.pop(0)
+    xs = [refs.pop(0) for _ in range(2 * chips)]
+    tags = [refs.pop(0) for _ in range(2 * chips)]
+    kvs = [refs.pop(0) for _ in range(chips)]
+    if first:
+        q_out, qt_out = refs.pop(0), refs.pop(0)
+    if last:
+        att_ref, ot_ref, lse_ref = refs.pop(0), refs.pop(0), refs.pop(0)
+    else:
+        acc_out, m_out = refs.pop(0), refs.pop(0)
+    s_scr, vt_scr = refs.pop(0), refs.pop(0)
+    rows = xs[0].shape[0]
+    half = wk_ref.shape[1]
+    heads = half // 64
+    queries = seg_ref.shape[1]
+    high = vt_scr.shape[1]
+    pair = 2 * rows
+    bias_q = bias_ref[layer : layer + 1, :]
+    bias_v = bias_k[layer : layer + 1, :]
+    for c in range(chips):
+        x = jnp.concatenate([xs[2 * c][...], xs[2 * c + 1][...]], axis=0)
+        if first:
+            q = (dot_nn(x, wq_ref[...]) + bias_q).astype(BF) * BF(0.125)
+            q_out[...] = q
+            qt_out[...] = q.T
+        kvs[c][:, :half] = dot_nn(x, wk_ref[...]).astype(BF)
+        values = (dot_nn(x, wv_ref[...]) + bias_v).astype(BF)
+        kvs[c][:, half:] = values
+        turned = values.T
+        for h in range(heads):
+            vt_scr[h, :64, c * pair : (c + 1) * pair] = turned[h * 64 : (h + 1) * 64]
+    vt_scr[:, 64:, :] = jnp.ones((heads, high - 64, chips * pair), BF)
+    qt = qt_out if first else qt_in
+    seg = seg_ref[...]
+    outs = []
+    if last:
+        lse_ref[...] = jnp.zeros_like(lse_ref)
+    else:
+        m_out[...] = jnp.zeros_like(m_out)
+    for h in range(heads):
+        qh = qt[h * 64 : (h + 1) * 64, :]
+        m8 = None
+        for b in range(2 * chips):
+            key = slice((b % 2) * rows, (b % 2 + 1) * rows)
+            scores = dot_nn(kvs[b // 2][key, h * 64 : (h + 1) * 64], qh)
+            ok = jnp.concatenate([tags[b][...]] * (queries // 128), axis=1) == seg
+            scores = jnp.where(ok, scores, LOW)
+            s_scr[h % 2, b * rows : (b + 1) * rows, :] = scores
+            top = jnp.max(scores.reshape(rows // 8, 8, queries), axis=0)
+            m8 = top if m8 is None else jnp.maximum(m8, top)
+        m = jnp.max(m8, axis=0, keepdims=True)
+        if not first:
+            m_old = m_in[h : h + 1, :]
+            m = jnp.maximum(m, m_old)
+        acc = jnp.zeros((high, queries), F32)
+        for b in range(2 * chips):
+            probs = jnp.exp(s_scr[h % 2, b * rows : (b + 1) * rows, :] - m).astype(BF)
+            acc = acc + dot_nn(vt_scr[h, :, b * rows : (b + 1) * rows], probs)
+        if not first:
+            acc = acc + acc_in[h] * jnp.exp(m_old - m)
+        if last:
+            total = acc[64:65]
+            out = acc[:64] / total
+            ot_ref[h * 64 : (h + 1) * 64, :] = out
+            lse_ref[h : h + 1, :] = m + jnp.log(total)
+            outs.append(out.astype(BF))
+        else:
+            acc_out[h] = acc
+            m_out[h : h + 1, :] = m
+    if last:
+        att_ref[...] = jnp.concatenate(outs, axis=0).T
+
+
+def tag_specs(tag_ids, rows):
+    return [pl.BlockSpec((None, rows, 128), lambda i, s, r=r: (r, 0, 0)) for r in tag_ids]
+
+
+def attend_call(layer, scal, state, seg_row, w_qkv, b_qv, xs, tags, tag_ids, last=False):
+    first = not state
+    rows, width = xs[0].shape
+    half = width // 2
+    heads = half // 64
+    queries = 2 * rows
+    chips = len(xs) // 2
+    high = 80
+    stat = sds((8, queries), F32)
+    out_shape = tuple(sds((2 * rows, width)) for _ in range(chips))
+    if first:
+        out_shape += (sds((queries, half)), sds((half, queries)))
+    if last:
+        out_shape += (sds((queries, half)), sds((half, queries), F32), stat)
+    else:
+        out_shape += (sds((heads, high, queries), F32), stat)
+
+    def weight(part):
+        return pl.BlockSpec((None, width, half), lambda i, s: (layer, 0, 2 * part + s[0] % 2))
+
+    def bias(part):
+        return pl.BlockSpec((LAYERS, half), lambda i, s: (0, 2 * part + s[0] % 2))
+
+    specs = [whole(a.shape) for a in state] + [whole(seg_row.shape), bias(0), weight(1), weight(2)]
+    args = tuple(state) + (seg_row, b_qv, w_qkv, w_qkv)
+    if first:
+        specs.append(weight(0))
+        args += (w_qkv,)
+    specs += [bias(1)] + [whole(x.shape) for x in xs] + tag_specs(tag_ids, rows)
+    args += (b_qv,) + tuple(xs) + (tags,) * len(xs)
+    return call(
+        functools.partial(attend_kernel, layer, chips, first, last),
+        "attend",
+        out_shape,
+        specs,
+        tuple(whole(o.shape) for o in out_shape),
+        (1,),
+        [
+            pltpu.VMEM((2, chips * 2 * rows, queries), F32),
+            pltpu.VMEM((heads, high, chips * 2 * rows), BF),
+        ],
+        chips * 12 * 4 * queries * half * rows,
+        args,
+        scal,
+    )
+
+
+def attend_back_kernel(blocks, adds, first, last, *refs):
+    refs = list(refs)
+    refs.pop(0)
+    if first:
+        b_m, b_o, w_out, ot_ref = (refs.pop(0) for _ in range(4))
+    else:
+        do_in, dot_in, corr_in, dq_in = (refs.pop(0) for _ in range(4))
+    q, qt, lse_ref, seg_ref = (refs.pop(0) for _ in range(4))
+    kvs = [refs.pop(0) for _ in range(blocks)]
+    more = [refs.pop(0) for _ in range(blocks)] if adds else None
+    tags = [refs.pop(0) for _ in range(blocks)]
+    outs = [refs.pop(0) for _ in range(blocks)]
+    if first:
+        do_out, dot_out, corr_out, dq_out = (refs.pop(0) for _ in range(4))
+    else:
+        dq_out = refs.pop(0)
+    dqt_scr = refs.pop(0)
+    rows, width = kvs[0].shape
+    half = width // 2
+    heads = half // 64
+    seg = seg_ref[...]
+    queries = seg.shape[1]
+    if first:
+        branch = jnp.concatenate([b_m[...], b_o[...]], axis=0)
+        grad_att = dot_nt(branch, w_out[...]).astype(BF)
+        do_out[...] = grad_att
+        turned = grad_att.T
+        dot_out[...] = turned
+        wide = turned.astype(F32) * ot_ref[...]
+        corr_out[...] = jnp.zeros_like(corr_out)
+        for h in range(heads):
+            corr_out[h : h + 1, :] = jnp.sum(wide[h * 64 : (h + 1) * 64], axis=0, keepdims=True)
+        do, dot, corr = do_out, dot_out, corr_out
+    else:
+        do, dot, corr = do_in, dot_in, corr_in
+    for b in range(blocks):
+        kt = kvs[b][:, :half].T
+        ok = jnp.concatenate([tags[b][...]] * (queries // 128), axis=1) == seg
+        dks, dvs = [], []
+        for h in range(heads):
+            sl = slice(h * 64, (h + 1) * 64)
+            vl = slice(half + h * 64, half + (h + 1) * 64)
+            scores = dot_nn(kvs[b][:, sl], qt[sl, :])
+            grad = dot_nn(kvs[b][:, vl], dot[sl, :])
+            probs = jnp.exp(jnp.where(ok, scores - lse_ref[h : h + 1, :], LOW))
+            grad = (probs * (grad - corr[h : h + 1, :])).astype(BF)
+            probs = probs.astype(BF)
+            term = dot_nn(kt[sl], grad)
+            if b == 0:
+                if first:
+                    dqt_scr[sl, :] = term
+                else:
+                    dqt_scr[sl, :] = dq_in[sl, :] + term
+            else:
+                dqt_scr[sl, :] += term
+            dks.append(dot_nn(grad, q[:, sl]))
+            dvs.append(dot_nn(probs, do[:, sl]))
+        result = jnp.concatenate(dks + dvs, axis=1)
+        if adds:
+            result = result + more[b][...].astype(F32)
+        outs[b][...] = result.astype(BF)
+    if last:
+        dq_out[...] = (dqt_scr[...] * 0.125).astype(BF).T
+    else:
+        dq_out[...] = dqt_scr[...]
+
+
+def attend_back_call(layer, scal, state, w_out, shared, kvs, adds, tags, tag_ids, last=False):
+    first = w_out is not None
+    rows = kvs[0].shape[0] // 2
+    width = kvs[0].shape[1]
+    half = width // 2
+    queries = 2 * rows
+    blocks = len(kvs)
+    out_shape = tuple(sds((rows, width)) for _ in range(blocks))
+    if first:
+        out_shape += (sds((queries, half)), sds((half, queries)), sds((8, queries), F32))
+    out_shape += (sds((queries, half)) if last else sds((half, queries), F32),)
+    args, specs = tuple(state), [whole(a.shape) for a in state]
+    if first:
+        args = args[:2] + (w_out,) + args[2:]
+        specs.insert(
+            2, pl.BlockSpec((None, half, width), lambda i, s: (layer, s[0] % 2, 0))
+        )
+    args += tuple(shared) + tuple(kvs) + tuple(adds or ())
+    specs += [whole(a.shape) for a in shared]
+    specs += [pl.BlockSpec((rows, width), lambda i, s, r=r: (r % 2, 0)) for r in tag_ids]
+    specs += [whole(a.shape) for a in adds or ()] + tag_specs(tag_ids, rows)
+    return call(
+        functools.partial(attend_back_kernel, blocks, adds is not None, first, last),
+        "attend_back",
+        out_shape,
+        specs,
+        tuple(whole(o.shape) for o in out_shape),
+        (1,),
+        [pltpu.VMEM((half, queries), F32)],
+        10 * 4 * queries * half * rows * blocks,
+        args + (tags,) * blocks,
+        scal,
+    )
+
+
+def normalize(hidden):
+    center = hidden - jnp.mean(hidden, axis=-1, keepdims=True)
+    spread = lax.rsqrt(jnp.mean(center * center, axis=-1, keepdims=True) + 1e-05)
+    return center * spread, spread
+
+
+def normalize_back(grad, unit, spread, gain):
+    scaled = grad * gain
+    mean = jnp.mean(scaled, axis=-1, keepdims=True)
+    along = jnp.mean(scaled * unit, axis=-1, keepdims=True)
+    return spread * (scaled - mean - unit * along)
+
+
+def gauss(up):
+    size = jnp.abs(up)
+    bell = jnp.exp(-0.5 * up * up)
+    t = 1.0 / (1.0 + 0.23164189 * size)
+    poly = 0.5307027145 * t - 0.7265760135
+    poly = poly * t + 0.7107068705
+    poly = poly * t - 0.142248368
+    poly = poly * t + 0.127414796
+    tail = poly * t * bell
+    return jnp.where(up < 0, tail, 1.0 - tail), bell
+
+
+def ffn_kernel(
+    layer, s, x, att, oatt, w_out, b_out, gain, shift, w_up, b_up, w_down, b_down,
+    unit1, rs1, normed, act, slope, unit2, rs2, y, total,
+):
+    n = pl.program_id(0)
+    rows = x.shape[0]
+    half = att.shape[1]
+    core = s[0] % 2
+
+    @pl.when(n == 0)
+    def _():
+        mine = pl.multiple_of(core * half, 128)
+        other = pl.multiple_of((1 - core) * half, 128)
+        branch = dot_nn(att[:rows], w_out[pl.ds(mine, half), :])
+        branch = branch + dot_nn(oatt[rows:], w_out[pl.ds(other, half), :])
+        first = x[...].astype(F32) + branch + b_out[layer : layer + 1, :]
+        unit, spread = normalize(first)
+        unit1[...] = unit
+        rs1[...] = jnp.broadcast_to(spread, rs1.shape)
+        low = (unit * gain[layer, 0:1, :] + shift[layer, 0:1, :]).astype(BF)
+        normed[...] = low
+        total[...] = low.astype(F32) + b_down[layer : layer + 1, :]
+
+    up = dot_nn(normed[...], w_up[...]) + b_up[layer : layer + 1, :]
+    phi, bell = gauss(up)
+    low = (up * phi).astype(BF)
+    act[...] = low
+    slope[...] = (phi + up * (0.3989422804014327 * bell)).astype(BF)
+    total[...] += dot_nn(low, w_down[...])
+
+    @pl.when(n == pl.num_programs(0) - 1)
+    def _():
+        unit, spread = normalize(total[...])
+        unit2[...] = unit
+        rs2[...] = jnp.broadcast_to(spread, rs2.shape)
+        y[...] = (unit * gain[layer, 1:2, :] + shift[layer, 1:2, :]).astype(BF)
+
+
+def ffn_call(layer, scal, x, att, oatt, w_out, b_out, gain, shift, w_up, b_up, w_down, b_down):
+    rows, width = x.shape
+    wide = w_up.shape[2]
+    steps = wide // width
+    vec = sds((rows, 128), F32)
+    out_shape = (
+        sds((rows, width), F32), vec, sds((rows, width)), sds((rows, wide)), sds((rows, wide)),
+        sds((rows, width), F32), vec, sds((rows, width)),
+    )
+    strip = pl.BlockSpec((rows, width), lambda n, s: (0, n))
+    return call(
+        functools.partial(ffn_kernel, layer),
+        "ffn",
+        out_shape,
+        [
+            whole(x.shape), whole(att.shape), whole(oatt.shape),
+            pl.BlockSpec((None, width, width), lambda n, s: (layer, 0, 0)),
+            whole(b_out.shape), whole(gain.shape), whole(shift.shape),
+            pl.BlockSpec((None, width, width), lambda n, s: (layer, 0, n)),
+            pl.BlockSpec((LAYERS, width), lambda n, s: (0, n)),
+            pl.BlockSpec((None, width, width), lambda n, s: (layer, n, 0)),
+            whole(b_down.shape),
+        ],
+        (
+            whole((rows, width)), whole((rows, 128)), whole((rows, width)), strip, strip,
+            whole((rows, width)), whole((rows, 128)), whole((rows, width)),
+        ),
+        (steps,),
+        [pltpu.VMEM((rows, width), F32)],
+        4 * rows * width * wide + 2 * rows * width * width,
+        (x, att, oatt, w_out, b_out, gain, shift, w_up, b_up, w_down, b_down),
+        scal,
+    )
+
+
+def ffn_back_kernel(
+    layer, s, gy, unit2, rs2, slope, unit1, rs1, gain, w_up, w_down,
+    d_down, d_up, d_branch, d_first, sums, total,
+):
+    n = pl.program_id(0)
+
+    @pl.when(n == 0)
+    def _():
+        grad = gy[...].astype(F32)
+        unit = unit2[...]
+        second = normalize_back(grad, unit, rs2[:, 0:1], gain[layer, 1:2, :])
+        sums[...] = jnp.zeros_like(sums)
+        sums[1:2, :] = jnp.sum(grad * unit, axis=0, keepdims=True)
+        sums[3:4, :] = jnp.sum(grad, axis=0, keepdims=True)
+        total[...] = second
+        low = second.astype(BF)
+        d_down[...] = low
+        sums[5:6, :] = jnp.sum(low.astype(F32), axis=0, keepdims=True)
+
+    low = (dot_nt(d_down[...], w_down[...]) * slope[...].astype(F32)).astype(BF)
+    d_up[...] = low
+    sums[pl.ds(6 + n, 1), :] = jnp.sum(low.astype(F32), axis=0, keepdims=True)
+    total[...] += dot_nt(low, w_up[...])
+
+    @pl.when(n == pl.num_programs(0) - 1)
+    def _():
+        grad = total[...]
+        unit = unit1[...]
+        first = normalize_back(grad, unit, rs1[:, 0:1], gain[layer, 0:1, :])
+        sums[0:1, :] = jnp.sum(grad * unit, axis=0, keepdims=True)
+        sums[2:3, :] = jnp.sum(grad, axis=0, keepdims=True)
+        d_first[...] = first
+        low = first.astype(BF)
+        d_branch[...] = low
+        sums[4:5, :] = jnp.sum(low.astype(F32), axis=0, keepdims=True)
+
+
+def ffn_back_call(layer, scal, gy, unit2, rs2, slope, unit1, rs1, gain, w_up, w_down):
+    rows, width = gy.shape
+    wide = w_up.shape[2]
+    steps = wide // width
+    low = sds((rows, width))
+    out_shape = (low, sds((rows, wide)), low, sds((rows, width), F32), sds((16, width), F32))
+    strip = pl.BlockSpec((rows, width), lambda n, s: (0, n))
+    out_specs = [whole(o.shape) for o in out_shape]
+    out_specs[1] = strip
+    return call(
+        functools.partial(ffn_back_kernel, layer),
+        "ffn_back",
+        out_shape,
+        [
+            whole(gy.shape), whole(unit2.shape), whole(rs2.shape), strip,
+            whole(unit1.shape), whole(rs1.shape), whole(gain.shape),
+            pl.BlockSpec((None, width, width), lambda n, s: (layer, 0, n)),
+            pl.BlockSpec((None, width, width), lambda n, s: (layer, n, 0)),
+        ],
+        tuple(out_specs),
+        (steps,),
+        [pltpu.VMEM((rows, width), F32)],
+        4 * rows * width * wide,
+        (gy, unit2, rs2, slope, unit1, rs1, gain, w_up, w_down),
+        scal,
+    )
+
+
+def input_back_kernel(s, d_first, dq, dkv, odq, odkv, w, gx):
+    rows = d_first.shape[0]
+    half = dq.shape[1]
+    width = 2 * half
+    core = s[0] % 2
+    result = d_first[...]
+    for at, q_part, kv_part in (
+        (core * half, dq[:rows], dkv),
+        ((1 - core) * half, odq[rows:], odkv),
+    ):
+        for i, part in enumerate((q_part, kv_part[:, :half], kv_part[:, half:])):
+            columns = pl.ds(pl.multiple_of(i * width + at, 128), half)
+            result = result + dot_nt(part, w[:, columns])
+    gx[...] = result
+
+
+def input_back_call(layer, scal, d_first, dq, dkv, odq, odkv, w_qkv):
+    rows, width = d_first.shape
+    strip = pl.BlockSpec((rows, 256), lambda n, s: (0, n))
+    return call(
+        input_back_kernel,
+        "input_back",
+        sds((rows, width), F32),
+        [
+            strip, whole(dq.shape), whole(dkv.shape), whole(odq.shape), whole(odkv.shape),
+            pl.BlockSpec((None, 256, 3 * width), lambda n, s: (layer, n, 0)),
+        ],
+        strip,
+        (width // 256,),
+        [],
+        6 * rows * width * width,
+        (d_first, dq, dkv, odq, odkv, w_qkv),
+        scal,
+    )
+
+
+def gather_rows(s, turned, picked, order):
+    chip, core = s[0] // 2, s[0] % 2
+    share = picked.shape[0] // len(order)
+    for at, step in enumerate(order):
+        begin = pl.multiple_of((chip ^ step) * (2 * share) + core * share, 32)
+        picked[at * share : (at + 1) * share, :] = turned[pl.ds(begin, share), :]
+
+
+def up_grad_kernel(s, x_m, x_o, g_m, g_o, keep, send, turned, picked):
+    rows = x_m.shape[0]
+
+    @pl.when(pl.program_id(0) == 0)
+    def _():
+        turned[:, :rows] = x_m[...].T
+        turned[:, rows:] = x_o[...].T
+        gather_rows(s, turned, picked, (0, 2, 1, 3))
+
+    grad = dot_nn(picked[:, :rows], g_m[...]) + dot_nn(picked[:, rows:], g_o[...])
+    share = picked.shape[0] // 4
+    for at in range(2):
+        keep[at] = grad[at * share : (at + 1) * share].astype(BF)
+        send[at] = grad[(2 + at) * share : (3 + at) * share].astype(BF)
+
+
+def up_grad_call(scal, x_m, x_o, g_m, g_o):
+    rows, width = x_m.shape
+    wide = g_m.shape[1]
+    steps = wide // width
+    share = width // 8
+    out = sds((2, steps * share, width))
+    strip = pl.BlockSpec((rows, width), lambda n, s: (0, n))
+    block = pl.BlockSpec((2, share, width), lambda n, s: (0, n, 0))
+    return call(
+        up_grad_kernel,
+        "up_grad",
+        (out, out),
+        [whole(x_m.shape), whole(x_o.shape), strip, strip],
+        (block, block),
+        (steps,),
+        [pltpu.VMEM((width, 2 * rows), BF), pltpu.VMEM((width // 2, 2 * rows), BF)],
+        2 * rows * width * wide,
+        (x_m, x_o, g_m, g_o),
+        scal,
+    )
+
+
+def down_grad_kernel(s, a_m, a_o, g_m, g_o, keep, send):
+    n = pl.program_id(0)
+    grad = dot_nn(a_m[...].T, g_m[...]) + dot_nn(a_o[...].T, g_o[...])
+    grad = grad.astype(BF)
+
+    @pl.when(n < 2)
+    def _():
+        keep[...] = grad
+
+    @pl.when(n >= 2)
+    def _():
+        send[...] = grad
+
+
+def down_grad_call(scal, a_m, a_o, g_m, g_o):
+    rows, wide = a_m.shape
+    width = g_m.shape[1]
+    share = wide // 8
+    out = sds((2, share, width))
+    picked = pl.BlockSpec((rows, share), lambda n, s: (0, 2 * ((s[0] // 2) ^ n) + s[0] % 2))
+    return call(
+        down_grad_kernel,
+        "down_grad",
+        (out, out),
+        [picked, picked, whole(g_m.shape), whole(g_o.shape)],
+        (
+            pl.BlockSpec((None, share, width), lambda n, s: (jnp.minimum(n, 1), 0, 0)),
+            pl.BlockSpec((None, share, width), lambda n, s: (jnp.maximum(n - 2, 0), 0, 0)),
+        ),
+        (4,),
+        [],
+        2 * rows * width * wide,
+        (a_m, a_o, g_m, g_o),
+        scal,
+    )
+
+
+def out_grad_kernel(
+    s, x_m, x_o, dq, dkv_m, dkv_r, odq, odkv_m, odkv_r, att, oatt, b_m, b_o, sums_m, sums_o,
+    keep_a, send_a, keep_b, send_b, turned, picked,
+):
+    rows, width = x_m.shape
+    half = width // 2
+    core = s[0] % 2
+    share = width // 8
+    mine = pl.ds(pl.multiple_of(core * half, 128), half)
+    other = pl.ds(pl.multiple_of((1 - core) * half, 128), half)
+    turned[:, :rows] = x_m[...].T
+    turned[:, rows:] = x_o[...].T
+    gather_rows(s, turned, picked, (0, 2, 1, 3))
+    left_m, left_o = picked[:, :rows], picked[:, rows:]
+
+    def put(refs, order, at, grad, columns):
+        for j in range(4):
+            place = order.index(j)
+            ref = refs[place // 2]
+            ref[place % 2, at * share : (at + 1) * share, columns] = grad[
+                (0, 2, 1, 3).index(j) * share : ((0, 2, 1, 3).index(j) + 1) * share
+            ].astype(BF)
+
+    first, second = (0, 2, 1, 3), (0, 1, 2, 3)
+    refs_a, refs_b = (keep_a, send_a), (keep_b, send_b)
+    for at, refs, order, place in (
+        (0, refs_a, first, 0),
+        (1, refs_a, first, 1),
+        (2, refs_b, second, 0),
+    ):
+        if at == 0:
+            pairs = ((dq[:rows], dq[rows:]), (odq[rows:], odq[:rows]))
+        else:
+            cut = slice((at - 1) * half, at * half)
+            pairs = ((dkv_m[:, cut], dkv_r[:, cut]), (odkv_r[:, cut], odkv_m[:, cut]))
+        for columns, (mine_rows, other_rows) in zip((mine, other), pairs):
+            grad = dot_nn(left_m, mine_rows) + dot_nn(left_o, other_rows)
+            put(refs, order, place, grad, columns)
+    turned[mine, :] = att[...].T
+    turned[other, :rows] = oatt[rows:].T
+    turned[other, rows:] = oatt[:rows].T
+    gather_rows(s, turned, picked, (0, 2, 1, 3))
+    grad = dot_nn(picked[:, :rows], b_m[...]) + dot_nn(picked[:, rows:], b_o[...])
+    put(refs_b, second, 1, grad, slice(0, width))
+    small = (sums_m[...] + sums_o[...]).astype(BF)
+    for ref in (keep_a, send_a, keep_b, send_b):
+        for at in range(2):
+            ref[at, 2 * share :, :] = small
+    for row, parts in ((10, (dq[...], odq[...])), (11, (dkv_m[:, half:], dkv_r[:, half:], odkv_m[:, half:], odkv_r[:, half:]))):
+        count = len(parts) // 2
+        for columns, group in ((mine, parts[:count]), (other, parts[count:])):
+            line = sum(jnp.sum(p.astype(F32), axis=0, keepdims=True) for p in group).astype(BF)
+            for ref in (keep_a, send_a, keep_b, send_b):
+                for at in range(2):
+                    ref[at, 2 * share + row : 2 * share + row + 1, columns] = line
+
+
+def out_grad_call(scal, *args):
+    rows, width = args[0].shape
+    share = width // 8
+    out = sds((2, 2 * share + 16, width))
+    return call(
+        out_grad_kernel,
+        "out_grad",
+        (out,) * 4,
+        [whole(a.shape) for a in args],
+        (whole(out.shape),) * 4,
+        (1,),
+        [pltpu.VMEM((width, 2 * rows), BF), pltpu.VMEM((width // 2, 2 * rows), BF)],
+        8 * rows * width * width,
+        args,
+        scal,
+    )
+
+
+def over_core(array):
+    return lax.ppermute(array, "seq", [(i, i ^ 1) for i in range(8)])
+
+
+def over_x(array):
+    return lax.ppermute(array, "seq", [(i, i ^ 2) for i in range(8)])
+
+
+def over_y(array):
+    return lax.ppermute(array, "seq", [(i, i ^ 4) for i in range(8)])
+
+
+def over_bucket(array, pairs):
+    return lax.ppermute(array, "bucket", pairs)
+
+
+def scatter_sum(keep_a, send_a, keep_b, send_b):
+    got_a, got_b = over_x(send_a), over_y(send_b)
+    pass_a = over_y(keep_a[1] + got_a[1])
+    pass_b = over_x(keep_b[1] + got_b[1])
+    return keep_a[0] + got_a[0] + pass_a, keep_b[0] + got_b[0] + pass_b
+
+
+def bucket_sum(part_a, part_b):
+    place = lax.axis_index("bucket")
+    outer = (place == 0) | (place == 3)
+    near = [(0, 1), (1, 0), (2, 3), (3, 2)]
+    far = [(0, 3), (3, 0), (1, 2), (2, 1)]
+    mine = jnp.where(outer, part_a, part_b) + over_bucket(jnp.where(outer, part_b, part_a), near)
+    mine = mine + over_bucket(mine, far)
+    other = over_bucket(mine, near)
+    return jnp.where(outer, mine, other), jnp.where(outer, other, mine)
+
+
+def fast_local(
+    frames, w_qkv, b_qv, w_out, b_out, ln_gain, ln_shift, w_up, b_up, w_down, b_down,
+    cotangent, clip_lengths, valid_lengths,
+):
+    rows, width = frames.shape[1:]
+    place = lax.axis_index("seq")
+    scal = place.astype(jnp.int32)[None]
+    blocks = place ^ jnp.arange(8, dtype=jnp.int32)
+    position = (blocks[:, None] * rows + jnp.arange(rows, dtype=jnp.int32)[None]).reshape(-1)
+    ends = jnp.cumsum(clip_lengths[0])
+    starts = ends - clip_lengths[0]
+    inside = (position[:, None] >= starts) & (position[:, None] < ends)
+    segment = jnp.sum(jnp.where(inside, jnp.arange(ends.shape[0], dtype=jnp.int32), 0), axis=1)
+    live = jnp.any(inside & (position[:, None] < starts + valid_lengths[0]), axis=1)
+    tags = jnp.where(live, segment, -1).reshape(8, rows, 1)
+    tags = jnp.broadcast_to(tags, (8, rows, 128))
+    seg_row = segment[: 2 * rows][None]
+
+    x = frames[0]
+    saved = []
+    for layer in range(LAYERS):
+        attend = functools.partial(attend_call, layer, scal)
+        x_r, x_x, x_y = over_core(x), over_x(x), over_y(x)
+        x_d = over_y(x_x)
+        x_xr, x_yr, x_dr = over_core(x_x), over_core(x_y), over_core(x_d)
+        kv, q, qt, acc, top = attend((), seg_row, w_qkv, b_qv, (x, x_r), tags, (0, 1))
+        kv_x, kv_y, acc, top = attend(
+            (qt, acc, top), seg_row, w_qkv, b_qv, (x_x, x_xr, x_y, x_yr), tags, (2, 3, 4, 5)
+        )
+        kv_d, att, ot, lse = attend(
+            (qt, acc, top), seg_row, w_qkv, b_qv, (x_d, x_dr), tags, (6, 7), last=True
+        )
+        oatt = over_core(att)
+        unit1, rs1, normed, act, slope, unit2, rs2, y = ffn_call(
+            layer, scal, x, att, oatt, w_out, b_out, ln_gain, ln_shift, w_up, b_up, w_down, b_down
+        )
+        saved.append(
+            (x, x_r, q, qt, kv, kv_x, kv_y, kv_d, att, oatt, ot, lse)
+            + (unit1, rs1, normed, over_core(normed), act, over_core(act), slope, unit2, rs2)
+        )
+        x = y
+    activations = x[None]
+
+    grad = cotangent[0]
+    ffn_parts, att_parts = [None] * LAYERS, [None] * LAYERS
+    for layer in reversed(range(LAYERS)):
+        x, x_r, q, qt, kv, kv_x, kv_y, kv_d, att, oatt, ot, lse = saved[layer][:12]
+        unit1, rs1, normed, o_normed, act, o_act, slope, unit2, rs2 = saved[layer][12:]
+        d_down, d_up, d_branch, d_first, sums = ffn_back_call(
+            layer, scal, grad, unit2, rs2, slope, unit1, rs1, ln_gain, w_up, w_down
+        )
+        o_branch = over_core(d_branch)
+        o_up, o_down, o_sums = over_core(d_up), over_core(d_down), over_core(sums)
+        keep_a, send_a = up_grad_call(scal, normed, o_normed, d_up, o_up)
+        keep_b, send_b = down_grad_call(scal, act, o_act, d_down, o_down)
+        ffn_parts[layer] = scatter_sum(keep_a, send_a, keep_b, send_b)
+        back = functools.partial(attend_back_call, layer, scal)
+        common = (q, qt, lse, seg_row)
+        g_dm, g_dr, do, dot, corr, dq = back(
+            (d_branch, o_branch, ot), w_out, common, (kv_d, kv_d), None, tags, (6, 7)
+        )
+        g_dm, g_dr = over_x(g_dm), over_y(g_dr)
+        g_xm, g_yr, dq = back(
+            (do, dot, corr, dq), None, common, (kv_x, kv_y), None, tags, (2, 5)
+        )
+        g_xm, g_yr = over_x(g_xm), over_y(g_yr)
+        g_ym, g_xr, dq = back(
+            (do, dot, corr, dq), None, common, (kv_y, kv_x), (g_dm, g_dr), tags, (4, 3)
+        )
+        g_ym, g_xr = over_y(g_ym), over_x(g_xr)
+        g_m, g_r, dq = back(
+            (do, dot, corr, dq), None, common, (kv, kv), (g_xm, g_yr), tags, (0, 1), last=True
+        )
+        g_m, g_r = g_m + g_ym, g_r + g_xr
+        odq, o_m, o_r = over_core(dq), over_core(g_m), over_core(g_r)
+        grad = input_back_call(layer, scal, d_first, dq, g_m, odq, o_r, w_qkv)
+        att_parts[layer] = scatter_sum(
+            *out_grad_call(
+                scal, x, x_r, dq, g_m, g_r, odq, o_m, o_r, att, oatt, d_branch, o_branch,
+                sums, o_sums,
+            )
+        )
+
+    share = width // 8
+    for layer in range(LAYERS):
+        ffn_parts[layer] = bucket_sum(*ffn_parts[layer])
+        att_parts[layer] = bucket_sum(*att_parts[layer])
+
+    def both(make):
+        return jnp.stack([make(layer).astype(F32) for layer in range(LAYERS)])
+
+    small = both(lambda l: att_parts[l][0][2 * share :])
+
+    def own(array, axis):
+        size = array.shape[axis] // 8
+        return lax.dynamic_slice_in_dim(array, place * size, size, axis)
+
+    def beside(array):
+        parts = array.shape[0] // share
+        return array.reshape(parts, share, width).transpose(1, 0, 2).reshape(share, -1)
+
+    return (
+        activations,
+        grad[None],
+        both(
+            lambda l: jnp.concatenate(
+                [beside(att_parts[l][0][: 2 * share]), att_parts[l][1][:share]], axis=1
+            )
+        ),
+        own(small[:, 10:12].reshape(LAYERS, -1), 1),
+        both(lambda l: att_parts[l][1][share : 2 * share]),
+        own(small[:, 4], 1),
+        own(small[:, 0:2], 2),
+        own(small[:, 2:4], 2),
+        both(lambda l: beside(ffn_parts[l][0])),
+        own(small[:, 6:10].reshape(LAYERS, -1), 1),
+        both(lambda l: ffn_parts[l][1]),
+        own(small[:, 5], 1),
+    )
 
 
 def clip_tags(lengths, valid, begin, count):
@@ -427,8 +1227,9 @@
         P("bucket", None),
         P("bucket", None),
     )
+    chips_2x2 = mesh.shape["seq"] == 8 and mesh.shape["bucket"] == 4
     return jax.shard_map(
-        local,
+        fast_local if chips_2x2 else local,
         mesh=mesh,
         in_specs=placed,
         out_specs=(

time: 1510 us -> 502 us (0.33)
  waiting for transfers between devices: 838 us -> 187 us
  matrix products: 270 us -> 0 us
  Pallas kernels: 0 us -> 150 us
  other arithmetic: 160 us -> 35.1 us
  local copies, waits for them, and re-layouts: 165 us -> 44.9 us
  starting transfers between devices: 1.5 us -> 72.7 us
  loops' own time: 24.7 us -> 0 us
    reduce_scatter x5 -> x0, waiting for transfers between devices: 321 us -> none  [the longest x2 116 us: attention_grads(): lax.psum_scatter(terms.reshape(count * rows, 2 * width).astype(jnp.bfloat...]
    unnamed x24 -> x0, waiting for transfers between devices: 280 us -> none
    dot_general x136 -> x0, matrix products: 270 us -> none  [the longest x16 40.6 us: attention_inner(): jnp.einsum('hqk,khd->qhd', grad_scores, key_heads, preferred_element_type...]
    ppermute x0 -> x74, waiting for transfers between devices: none -> 187 us  [the longest x18 63.1 us: over_y(): return lax.ppermute(array, 'seq', [(i, i ^ 4) for i in range(8)])]
    pallas_call x0 -> x26, Pallas kernels: none -> 150 us  [call(): pl.pallas_call(body, name=name, out_shape=out_shape, grid_spec=pltpu.Pref...]
    psum x1 -> x0, waiting for transfers between devices: 122 us -> none  [local(): lax.psum(s_wqkv.astype(jnp.bfloat16), 'bucket').astype(jnp.float32)]
    all_gather x4 -> x0, waiting for transfers between devices: 116 us -> none  [the longest x2 59.7 us: forward_layer(): value_piece = lax.all_gather(values, 'seq', axis=0, tiled=True)]
    ppermute x0 -> x74, starting transfers between devices: none -> 72.7 us  [the longest x18 24.4 us: over_y(): return lax.ppermute(array, 'seq', [(i, i ^ 4) for i in range(8)])]
  transfers between devices with their start and end apart: 17 -> 74, of which waited for: 17 -> 31; matrix products, arithmetic and copies ran while one was open for 6% -> 7% of each run, Pallas kernels for 0% -> 20%
where the time goes in v1:
time: 502 us; the launch traced here: 492 us
  waiting for transfers between devices  187 us (37%)
  Pallas kernels  150 us (30%)
  starting transfers between devices  72.7 us (14%)
  local copies, waits for them, and re-layouts  44.9 us (9%)
  other arithmetic  35.1 us (7%)
    pallas_call x26, Pallas kernels, call(): pl.pallas_call(body, name=name, out_shape=out_shape, grid_spec=pltpu.Pref...  150 us
    ppermute x18, waiting for transfers between devices, over_y(): return lax.ppermute(array, 'seq', [(i, i ^ 4) for i in range(8)])  63.1 us
    ppermute x16, waiting for transfers between devices, over_x(): return lax.ppermute(array, 'seq', [(i, i ^ 2) for i in range(8)])  60.4 us
    ppermute x12, waiting for transfers between devices, over_bucket(): return lax.ppermute(array, 'bucket', pairs)  56.8 us
    unnamed x267, local copies, waits for them, and re-layouts  39.1 us
    ppermute x18, starting transfers between devices, over_y(): return lax.ppermute(array, 'seq', [(i, i ^ 4) for i in range(8)])  24.4 us
    ppermute x12, starting transfers between devices, over_bucket(): return lax.ppermute(array, 'bucket', pairs)  23.4 us
    ppermute x16, starting transfers between devices, over_x(): return lax.ppermute(array, 'seq', [(i, i ^ 2) for i in range(8)])  19.6 us
  transfers between devices with their start and end apart: 74, of which 31 were waited for; matrix products, arithmetic and copies ran while one was open for 7% of the time, Pallas kernels for 20%

profile of v1, /device:TPU:0, one launch (start us, length us, event | category | flops | bytes accessed | tf_op | source)
XLA Modules:
  0.0 492.4 jit_solution(17644808255414640492)
XLA Ops:
  1.2 2.6 collective-permute-start.1
  7.1 6.6 %collective-permute-done.1.refs_9_ = bf16[256,768]{1,0:T(8,128)(2,1)S(1)} collective-permute-done((bf16[256,768]{1,0:T(8,128)(2,1)}, bf16[256,768]{1,0:T(8,128)(2,1)S(1)}, u32[]{:S(2)}, u32[]{:S(2)}) %collective-permute-start.1) | collective-permute-done | bytes 393248 | tf_op jit(solution)/shard_map/ppermute | solution.py:660
  16.1 3.0 copy-done
  19.1 4.3 attend.6
  25.4 6.8 %attend.7 = (bf16[512,768]{1,0:T(8,128)(2,1)S(1)}, bf16[512,768]{1,0:T(8,128)(2,1)S(1)}, f32[6,80,512]{2,1,0:T(8,128)S(1)}, f32[8,512]{1,0:T(8,128)S(1)}) custom-call(s32[1]{0:T(128)} %bitcast.refs_0_.s, bf16[384,512]{1,0:T(8,128)(2,1)S(1)} %get-tuple-element.110.refs_1_.refs_6_, f32[6,80,512]{2,1,0:T(8,128)S(1)} %get-tuple-element.111.refs_2_, ...), custom_call_target="tpu_custom_call" | custom-call | flops 4831838208 | bytes 7716864 | tf_op jit(solution)/shard_map/attend/pallas_call | solution.py:38
  33.2 5.8 %attend.8 = (bf16[512,768]{1,0:T(8,128)(2,1)S(1)}, bf16[512,384]{1,0:T(8,128)(2,1)S(1)}, f32[384,512]{1,0:T(8,128)S(1)}, f32[8,512]{1,0:T(8,128)S(1)}) custom-call(s32[1]{0:T(128)} %bitcast.refs_0_.s, bf16[384,512]{1,0:T(8,128)(2,1)S(1)} %get-tuple-element.110.refs_1_.refs_6_, f32[6,80,512]{2,1,0:T(8,128)S(1)} %get-tuple-element.113.refs_2_, ...), custom_call_target="tpu_custom_call" | custom-call | flops 2415919104 | bytes 5947392 | tf_op jit(solution)/shard_map/attend/pallas_call | solution.py:38
  42.8 3.7 copy-done.2
  46.4 7.9 %ffn.2 = (f32[256,768]{1,0:T(8,128)S(1)}, f32[256,128]{1,0:T(8,128)S(1)}, bf16[256,768]{1,0:T(8,128)(2,1)S(1)}, bf16[256,3072]{1,0:T(8,128)(2,1)}, bf16[256,3072...) custom-call(s32[1]{0:T(128)} %bitcast.refs_0_.s, ...), custom_call_target="tpu_custom_call" | custom-call | flops 2717908992 | bytes 17301504 | tf_op jit(solution)/shard_map/ffn/pallas_call | solution.py:38
  58.4 8.1 %collective-permute-done.9.refs_9_ = bf16[256,768]{1,0:T(8,128)(2,1)S(1)} collective-permute-done((bf16[256,768]{1,0:T(8,128)(2,1)S(1)}, bf16[256,768]{1,0:T(8,128)(2,1)S(1)}, u32[]{:S(2)}, u32[]{:S(2)}) %collective-permute-start.9) | collective-permute-done | bytes 393248 | tf_op jit(solution)/shard_map/ppermute | solution.py:660
  68.8 4.3 attend.9
  73.9 3.2 collective-permute-done.13.refs_9_
  77.1 6.8 %attend.10 = (bf16[512,768]{1,0:T(8,128)(2,1)S(1)}, bf16[512,768]{1,0:T(8,128)(2,1)S(1)}, f32[6,80,512]{2,1,0:T(8,128)S(1)}, f32[8,512]{1,0:T(8,128)S(1)}) custom-call(s32[1]{0:T(128)} %bitcast.refs_0_.s, bf16[384,512]{1,0:T(8,128)(2,1)S(1)} %get-tuple-element.117.refs_1_.refs_6_, f32[6,80,512]{2,1,0:T(8,128)S(1)} %get-tuple-element.118.refs_2_, ...), custom_call_target="tpu_custom_call" | custom-call | flops 4831838208 | bytes 7716864 | tf_op jit(solution)/shard_map/attend/pallas_call | solution.py:38
  84.9 16.7 %attend.11 = (bf16[512,768]{1,0:T(8,128)(2,1)S(1)}, bf16[512,384]{1,0:T(8,128)(2,1)S(1)}, f32[384,512]{1,0:T(8,128)S(1)}, f32[8,512]{1,0:T(8,128)S(1)}) custom-call(s32[1]{0:T(128)} %bitcast.refs_0_.s, bf16[384,512]{1,0:T(8,128)(2,1)S(1)} %get-tuple-element.117.refs_1_.refs_6_, f32[6,80,512]{2,1,0:T(8,128)S(1)} %get-tuple-element.120.refs_2_, ...), custom_call_target="tpu_custom_call" | custom-call | flops 2415919104 | bytes 5947392 | tf_op jit(solution)/shard_map/attend/pallas_call | solution.py:38
  106.0 3.7 copy-done.3
  109.6 8.2 %ffn.3 = (f32[256,768]{1,0:T(8,128)S(1)}, f32[256,128]{1,0:T(8,128)S(1)}, bf16[256,768]{1,0:T(8,128)(2,1)}, bf16[256,3072]{1,0:T(8,128)(2,1)}, bf16[256,3072]{1,...) custom-call(s32[1]{0:T(128)} %bitcast.refs_0_.s, ...), custom_call_target="tpu_custom_call" | custom-call | flops 2717908992 | bytes 17301504 | tf_op jit(solution)/shard_map/ffn/pallas_call | solution.py:38
  118.7 3.7 copy-done.4
  122.4 3.7 copy-done.6
  127.2 6.3 %ffn_back.2 = (bf16[256,768]{1,0:T(8,128)(2,1)}, bf16[256,3072]{1,0:T(8,128)(2,1)}, bf16[256,768]{1,0:T(8,128)(2,1)S(1)}, f32[256,768]{1,0:T(8,128)S(1)}, f32[16,768]{1,0:T(8,128)S(1)}) custom-call(s32[1]{0:T(128)} %bitcast.refs_0_.s, bf16[256,768]{1,0:T(8,128)(2,1)S(1)} %bitcast.151, f32[256,768]{1,0:T(8,128)S(1)} %get-tuple-element.124.unit2, ...), custom_call_target="tpu_custom_call" | custom-call | flops 2415919104 | bytes 9584640 | tf_op jit(solution)/shard_map/ffn_back/pallas_call | solution.py:38
  135.3 6.0 %attend_back.8 = (bf16[256,768]{1,0:T(8,128)(2,1)S(1)}, bf16[256,768]{1,0:T(8,128)(2,1)S(1)}, bf16[512,384]{1,0:T(8,128)(2,1)S(1)}, bf16[384,512]{1,0:T(8,128)(2...) custom-call(s32[1]{0:T(128)} %bitcast.refs_0_.s, bf16[256,768]{1,0:T(8,128)(2,1)S(1)} %get-tuple-element.130.refs_1_.b_m, ...), custom_call_target="tpu_custom_call" | custom-call | flops 4026531840 | bytes 7127040 | tf_op jit(solution)/shard_map/attend_back/pallas_call | solution.py:38
  144.6 5.6 %attend_back.9 = (bf16[256,768]{1,0:T(8,128)(2,1)S(1)}, bf16[256,768]{1,0:T(8,128)(2,1)S(1)}, f32[384,512]{1,0:T(8,128)S(1)}) custom-call(s32[1]{0:T(128)} %bitcast.refs_0_.s, bf16[512,384]{1,0:T(8,128)(2,1)S(1)} %get-tuple-element.135.refs_1_, bf16[384,512]{1,0:T(8,128)(2,1)S(1)} %get-tuple-element.136.refs_2_, f32[8,512]{1,0:T(8,128)S(1)} %get-tuple-element.137.refs_3_, ...), custom_call_target="tpu_custom_call" | custom-call | flops 4026531840 | bytes 4718592 | tf_op jit(solution)/shard_map/attend_back/pallas_call | solution.py:38
  152.8 2.3 collective-permute-done.18.refs_12_
  155.1 6.1 %attend_back.10 = (bf16[256,768]{1,0:T(8,128)(2,1)S(1)}, bf16[256,768]{1,0:T(8,128)(2,1)S(1)}, f32[384,512]{1,0:T(8,128)S(1)}) custom-call(s32[1]{0:T(128)} %bitcast.refs_0_.s, bf16[512,384]{1,0:T(8,128)(2,1)S(1)} %get-tuple-element.135.refs_1_, bf16[384,512]{1,0:T(8,128)(2,1)S(1)} %get-tuple-element.136.refs_2_, f32[8,512]{1,0:T(8,128)S(1)} %get-tuple-element.137.refs_3_, ...), custom_call_target="tpu_custom_call" | custom-call | flops 4026531840 | bytes 4718592 | tf_op jit(solution)/shard_map/attend_back/pallas_call | solution.py:38
  161.3 2.0 collective-permute-start.21
  163.3 5.7 %attend_back.11 = (bf16[256,768]{1,0:T(8,128)(2,1)S(1)}, bf16[256,768]{1,0:T(8,128)(2,1)S(1)}, bf16[512,384]{1,0:T(8,128)(2,1)S(1)}) custom-call(s32[1]{0:T(128)} %bitcast.refs_0_.s, bf16[512,384]{1,0:T(8,128)(2,1)S(1)} %get-tuple-element.135.refs_1_, bf16[384,512]{1,0:T(8,128)(2,1)S(1)} %get-tuple-element.136.refs_2_, ...), custom_call_target="tpu_custom_call" | custom-call | flops 4026531840 | bytes 3538944 | tf_op jit(solution)/shard_map/attend_back/pallas_call | solution.py:38
  175.7 3.1 input_back.2.gy
  179.3 3.7 copy-done.5
  183.0 6.4 %ffn_back.3 = (bf16[256,768]{1,0:T(8,128)(2,1)S(1)}, bf16[256,3072]{1,0:T(8,128)(2,1)S(1)}, bf16[256,768]{1,0:T(8,128)(2,1)}, f32[256,768]{1,0:T(8,128)S(1)}, f32[16,768]{1,0:T(8,128)S(1)}) custom-call(s32[1]{0:T(128)} %bitcast.refs_0_.s, f32[256,768]{1,0:T(8,128)S(1)} %input_back.2.gy, f32[256,768]{1,0:T(8,128)S(1)} %copy-done.51, ...), custom_call_target="tpu_custom_call" | custom-call | flops 2415919104 | bytes 9584640 | tf_op jit(solution)/shard_map/ffn_back/pallas_call | solution.py:38
  196.0 3.9 down_grad.3
  202.3 4.4 up_grad.3
  206.9 3.8 out_grad.3
  213.1 7.1 %attend_back.12 = (bf16[256,768]{1,0:T(8,128)(2,1)S(1)}, bf16[256,768]{1,0:T(8,128)(2,1)S(1)}, bf16[512,384]{1,0:T(8,128)(2,1)S(1)}, bf16[384,512]{1,0:T(8,128)(...) custom-call(s32[1]{0:T(128)} %bitcast.refs_0_.s, bf16[256,768]{1,0:T(8,128)(2,1)} %get-tuple-element.159.refs_1_.b_m, ...), custom_call_target="tpu_custom_call" | custom-call | flops 4026531840 | bytes 7127040 | tf_op jit(solution)/shard_map/attend_back/pallas_call | solution.py:38
  222.0 4.1 down_grad.2
  226.1 5.7 %attend_back.13 = (bf16[256,768]{1,0:T(8,128)(2,1)S(1)}, bf16[256,768]{1,0:T(8,128)(2,1)S(1)}, f32[384,512]{1,0:T(8,128)S(1)}) custom-call(s32[1]{0:T(128)} %bitcast.refs_0_.s, bf16[512,384]{1,0:T(8,128)(2,1)S(1)} %get-tuple-element.164.refs_1_, bf16[384,512]{1,0:T(8,128)(2,1)S(1)} %get-tuple-element.165.refs_2_, f32[8,512]{1,0:T(8,128)S(1)} %get-tuple-element.166.refs_3_, ...), custom_call_target="tpu_custom_call" | custom-call | flops 4026531840 | bytes 4718592 | tf_op jit(solution)/shard_map/attend_back/pallas_call | solution.py:38
  231.8 4.3 collective-permute-done.26.refs_11_
  236.1 14.6 %collective-permute-done.27.refs_12_ = bf16[256,768]{1,0:T(8,128)(2,1)S(1)} collective-permute-done((bf16[256,768]{1,0:T(8,128)(2,1)S(1)}, bf16[256,768]{1,0:T(8,128)(2,1)S(1)}, u32[]{:S(2)}, u32[]{:S(2)}) %collective-permute-start.27) | collective-permute-done | bytes 393248 | tf_op jit(solution)/shard_map/ppermute | solution.py:664
  252.3 5.7 %attend_back.14 = (bf16[256,768]{1,0:T(8,128)(2,1)S(1)}, bf16[256,768]{1,0:T(8,128)(2,1)S(1)}, f32[384,512]{1,0:T(8,128)S(1)}) custom-call(s32[1]{0:T(128)} %bitcast.refs_0_.s, bf16[512,384]{1,0:T(8,128)(2,1)S(1)} %get-tuple-element.164.refs_1_, bf16[384,512]{1,0:T(8,128)(2,1)S(1)} %get-tuple-element.165.refs_2_, f32[8,512]{1,0:T(8,128)S(1)} %get-tuple-element.166.refs_3_, ...), custom_call_target="tpu_custom_call" | custom-call | flops 4026531840 | bytes 4718592 | tf_op jit(solution)/shard_map/attend_back/pallas_call | solution.py:38
  261.3 2.5 collective-permute-start.65
  263.8 6.4 %collective-permute-done.29.refs_12_ = bf16[256,768]{1,0:T(8,128)(2,1)S(1)} collective-permute-done((bf16[256,768]{1,0:T(8,128)(2,1)S(1)}, bf16[256,768]{1,0:T(8,128)(2,1)S(1)}, u32[]{:S(2)}, u32[]{:S(2)}) %collective-permute-start.29) | collective-permute-done | bytes 393248 | tf_op jit(solution)/shard_map/ppermute | solution.py:664
  272.2 4.4 collective-permute-done.30
  278.1 6.1 %attend_back.15 = (bf16[256,768]{1,0:T(8,128)(2,1)S(1)}, bf16[256,768]{1,0:T(8,128)(2,1)S(1)}, bf16[512,384]{1,0:T(8,128)(2,1)S(1)}) custom-call(s32[1]{0:T(128)} %bitcast.refs_0_.s, bf16[512,384]{1,0:T(8,128)(2,1)S(1)} %get-tuple-element.164.refs_1_, bf16[384,512]{1,0:T(8,128)(2,1)S(1)} %get-tuple-element.165.refs_2_, ...), custom_call_target="tpu_custom_call" | custom-call | flops 4026531840 | bytes 3538944 | tf_op jit(solution)/shard_map/attend_back/pallas_call | solution.py:38
  284.4 17.1 %collective-permute-done.48 = bf16[208,768]{1,0:T(8,128)(2,1)S(1)} collective-permute-done((bf16[208,768]{1,0:T(8,128)(2,1)S(1)}, bf16[208,768]{1,0:T(8,128)(2,1)S(1)}, u32[]{:S(2)}, u32[]{:S(2)}) %collective-permute-start.48) | collective-permute-done | bytes 319520 | tf_op jit(solution)/shard_map/ppermute | solution.py:660
  307.1 3.3 out_grad.2
  311.2 3.7 collective-permute-done.49
  318.6 3.4 up_grad.2
  322.0 24.4 %collective-permute-done.38 = bf16[2,208,768]{2,1,0:T(8,128)(2,1)S(1)} collective-permute-done((bf16[2,208,768]{2,1,0:T(8,128)(2,1)S(1)}, bf16[2,208,768]{2,1,0:T(8,128)(2,1)S(1)}, u32[]{:S(2)}, u32[]{:S(2)}) %collective-permute-start.38) | collective-permute-done | bytes 639008 | tf_op jit(solution)/shard_map/ppermute | solution.py:664
  346.3 3.6 collective-permute-start.50
  353.5 4.7 collective-permute-done.66
  363.6 2.1 fusion.6
  368.3 18.4 %collective-permute-done.39 = bf16[208,768]{1,0:T(8,128)(2,1)} collective-permute-done((bf16[208,768]{1,0:T(8,128)(2,1)}, bf16[208,768]{1,0:T(8,128)(2,1)}, u32[]{:S(2)}, u32[]{:S(2)}) %collective-permute-start.39) | collective-permute-done | bytes 319520 | tf_op jit(solution)/shard_map/ppermute | solution.py:660
  388.2 2.1 collective-permute-start.40
  390.3 3.1 select_add_fusion
  393.7 2.1 fusion.9
  397.5 16.1 %collective-permute-done.40 = bf16[208,768]{1,0:T(8,128)(2,1)S(1)} collective-permute-done((bf16[208,768]{1,0:T(8,128)(2,1)S(1)}, bf16[208,768]{1,0:T(8,128)(2,1)S(1)}, u32[]{:S(2)}, u32[]{:S(2)}) %collective-permute-start.40) | collective-permute-done | bytes 319520 | tf_op jit(solution)/shard_map/ppermute | solution.py:668
  413.6 2.0 select_add_fusion.3
  415.7 2.8 input_back.3
  422.0 3.1 collective-permute-start.73
  425.1 3.2 collective-permute-done.41
  430.9 2.5 broadcast_select_fusion.3
  433.9 12.6 %collective-permute-done.42 = bf16[208,768]{1,0:T(8,128)(2,1)S(1)} collective-permute-done((bf16[208,768]{1,0:T(8,128)(2,1)S(1)}, bf16[208,768]{1,0:T(8,128)(2,1)S(1)}, u32[]{:S(2)}, u32[]{:S(2)}) %collective-permute-start.42) | collective-permute-done | bytes 319520 | tf_op jit(solution)/shard_map/ppermute | solution.py:668
  449.9 5.7 %collective-permute-done.60 = bf16[384,768]{1,0:T(8,128)(2,1)} collective-permute-done((bf16[384,768]{1,0:T(8,128)(2,1)}, bf16[384,768]{1,0:T(8,128)(2,1)}, u32[]{:S(2)}, u32[]{:S(2)}) %collective-permute-start.60) | collective-permute-done | bytes 589856 | tf_op jit(solution)/shard_map/ppermute | solution.py:668
  455.6 2.0 select_add_fusion.1
  459.8 9.5 %collective-permute-done.61 = bf16[384,768]{1,0:T(8,128)(2,1)S(1)} collective-permute-done((bf16[384,768]{1,0:T(8,128)(2,1)S(1)}, bf16[384,768]{1,0:T(8,128)(2,1)S(1)}, u32[]{:S(2)}, u32[]{:S(2)}) %collective-permute-start.61) | collective-permute-done | bytes 589856 | tf_op jit(solution)/shard_map/ppermute | solution.py:668
  469.6 9.2 %collective-permute-start.62 = (bf16[384,768]{1,0:T(8,128)(2,1)S(1)}, bf16[384,768]{1,0:T(8,128)(2,1)S(1)}, u32[]{:S(2)}, u32[]{:S(2)}) collective-permute-start(bf16[384,768]{1,0:T(8,128)(2,1)S(1)} %add.238), channel_id=1, source_target_pairs={{0,8},{8,0},{16,24},{24,16},{1,9},{9,1},{17,25},{25,17},{2,10},{10... | collective-permute-start | bytes 1769480 | tf_op jit(solution)/shard_map/ppermute | solution.py:668
  482.1 6.1 %collective-permute-done.62 = bf16[384,768]{1,0:T(8,128)(2,1)S(1)} collective-permute-done((bf16[384,768]{1,0:T(8,128)(2,1)S(1)}, bf16[384,768]{1,0:T(8,128)(2,1)S(1)}, u32[]{:S(2)}, u32[]{:S(2)}) %collective-permute-start.62) | collective-permute-done | bytes 589856 | tf_op jit(solution)/shard_map/ppermute | solution.py:668
  (441 shorter events, 108.7 us)
Async XLA Ops:
  0.7 15.0 %collective-permute-start = (bf16[256,768]{1,0:T(8,128)(2,1)}, bf16[256,768]{1,0:T(8,128)(2,1)S(1)}, u32[]{:S(2)}, u32[]{:S(2)}) collective-permute-start(bf16[256,768]{1,0:T(8,128)(2,1)} %bitcast.145), channel_id=1, source_target_pairs={{0,1},{1,0},{2,3},{3,2},{4,5},{5,4},{6,7},{7,6},{8,9},{9,8},{10,11... | collective-permute-start | bytes 1179656 | tf_op jit(solution)/shard_map/ppermute | solution.py:656
  1.2 12.5 %collective-permute-start.1 = (bf16[256,768]{1,0:T(8,128)(2,1)}, bf16[256,768]{1,0:T(8,128)(2,1)S(1)}, u32[]{:S(2)}, u32[]{:S(2)}) collective-permute-start(bf16[256,768]{1,0:T(8,128)(2,1)} %bitcast.146), channel_id=1, source_target_pairs={{0,2},{1,3},{2,0},{3,1},{4,6},{5,7},{6,4},{7,5},{8,10},{9,11},{10,... | collective-permute-start | bytes 1179656 | tf_op jit(solution)/shard_map/ppermute | solution.py:660
  3.8 11.7 %collective-permute-start.3 = (bf16[256,768]{1,0:T(8,128)(2,1)}, bf16[256,768]{1,0:T(8,128)(2,1)S(1)}, u32[]{:S(2)}, u32[]{:S(2)}) collective-permute-start(bf16[256,768]{1,0:T(8,128)(2,1)} %bitcast.147), channel_id=1, source_target_pairs={{0,4},{1,5},{2,6},{3,7},{4,0},{5,1},{6,2},{7,3},{8,12},{9,13},{10,... | collective-permute-start | bytes 1179656 | tf_op jit(solution)/shard_map/ppermute | solution.py:664
  13.7 11.7 %collective-permute-start.2 = (bf16[256,768]{1,0:T(8,128)(2,1)S(1)}, bf16[256,768]{1,0:T(8,128)(2,1)S(1)}, u32[]{:S(2)}, u32[]{:S(2)}) collective-permute-start(bf16[256,768]{1,0:T(8,128)(2,1)S(1)} %collective-permute-done.1.refs_9_), channel_id=1, source_target_pairs={{0,1},{1,0},{2,3},{3,2},{4,5},{5,4},{6,7},{7,6},{8,9},{9,8},{10,11... | collective-permute-start | bytes 1179656 | tf_op jit(solution)/shard_map/ppermute | solution.py:656
  13.7 11.7 %collective-permute-start.5 = (bf16[256,768]{1,0:T(8,128)(2,1)S(1)}, bf16[256,768]{1,0:T(8,128)(2,1)}, u32[]{:S(2)}, u32[]{:S(2)}) collective-permute-start(bf16[256,768]{1,0:T(8,128)(2,1)S(1)} %collective-permute-done.1.refs_9_), channel_id=1, source_target_pairs={{0,4},{1,5},{2,6},{3,7},{4,0},{5,1},{6,2},{7,3},{8,12},{9,13},{10,... | collective-permute-start | bytes 1179656 | tf_op jit(solution)/shard_map/ppermute | solution.py:664
  15.5 9.9 %collective-permute-start.4 = (bf16[256,768]{1,0:T(8,128)(2,1)S(1)}, bf16[256,768]{1,0:T(8,128)(2,1)S(1)}, u32[]{:S(2)}, u32[]{:S(2)}) collective-permute-start(bf16[256,768]{1,0:T(8,128)(2,1)S(1)} %collective-permute-done.3.refs_11_), channel_id=1, source_target_pairs={{0,1},{1,0},{2,3},{3,2},{4,5},{5,4},{6,7},{7,6},{8,9},{9,8},{10,11... | collective-permute-start | bytes 1179656 | tf_op jit(solution)/shard_map/ppermute | solution.py:656
  25.3 7.7 %collective-permute-start.6 = (bf16[256,768]{1,0:T(8,128)(2,1)}, bf16[256,768]{1,0:T(8,128)(2,1)S(1)}, u32[]{:S(2)}, u32[]{:S(2)}) collective-permute-start(bf16[256,768]{1,0:T(8,128)(2,1)} %collective-permute-done.5.refs_9_), channel_id=1, source_target_pairs={{0,1},{1,0},{2,3},{3,2},{4,5},{5,4},{6,7},{7,6},{8,9},{9,8},{10,11... | collective-permute-start | bytes 1179656 | tf_op jit(solution)/shard_map/ppermute | solution.py:656
  55.1 11.4 %collective-permute-start.9 = (bf16[256,768]{1,0:T(8,128)(2,1)S(1)}, bf16[256,768]{1,0:T(8,128)(2,1)S(1)}, u32[]{:S(2)}, u32[]{:S(2)}) collective-permute-start(bf16[256,768]{1,0:T(8,128)(2,1)S(1)} %get-tuple-element.116.refs_7_.x.x_m), channel_id=1, source_target_pairs={{0,2},{1,3},{2,0},{3,1},{4,6},{5,7},{6,4},{7,5},{8,10},{9,11},{10,... | collective-permute-start | bytes 1179656 | tf_op jit(solution)/shard_map/ppermute | solution.py:660
  56.9 11.4 %collective-permute-start.11 = (bf16[256,768]{1,0:T(8,128)(2,1)S(1)}, bf16[256,768]{1,0:T(8,128)(2,1)S(1)}, u32[]{:S(2)}, u32[]{:S(2)}) collective-permute-start(bf16[256,768]{1,0:T(8,128)(2,1)S(1)} %get-tuple-element.116.refs_7_.x.x_m), channel_id=1, source_target_pairs={{0,4},{1,5},{2,6},{3,7},{4,0},{5,1},{6,2},{7,3},{8,12},{9,13},{10,... | collective-permute-start | bytes 1179656 | tf_op jit(solution)/shard_map/ppermute | solution.py:664
  58.4 10.4 %collective-permute-start.8 = (bf16[256,768]{1,0:T(8,128)(2,1)S(1)}, bf16[256,768]{1,0:T(8,128)(2,1)S(1)}, u32[]{:S(2)}, u32[]{:S(2)}) collective-permute-start(bf16[256,768]{1,0:T(8,128)(2,1)S(1)} %get-tuple-element.116.refs_7_.x.x_m), channel_id=1, source_target_pairs={{0,1},{1,0},{2,3},{3,2},{4,5},{5,4},{6,7},{7,6},{8,9},{9,8},{10,11... | collective-permute-start | bytes 1179656 | tf_op jit(solution)/shard_map/ppermute | solution.py:656
  66.5 10.6 %collective-permute-start.13 = (bf16[256,768]{1,0:T(8,128)(2,1)S(1)}, bf16[256,768]{1,0:T(8,128)(2,1)S(1)}, u32[]{:S(2)}, u32[]{:S(2)}) collective-permute-start(bf16[256,768]{1,0:T(8,128)(2,1)S(1)} %collective-permute-done.9.refs_9_), channel_id=1, source_target_pairs={{0,4},{1,5},{2,6},{3,7},{4,0},{5,1},{6,2},{7,3},{8,12},{9,13},{10,... | collective-permute-start | bytes 1179656 | tf_op jit(solution)/shard_map/ppermute | solution.py:664
  68.3 8.8 %collective-permute-start.10 = (bf16[256,768]{1,0:T(8,128)(2,1)S(1)}, bf16[256,768]{1,0:T(8,128)(2,1)S(1)}, u32[]{:S(2)}, u32[]{:S(2)}) collective-permute-start(bf16[256,768]{1,0:T(8,128)(2,1)S(1)} %collective-permute-done.9.refs_9_), channel_id=1, source_target_pairs={{0,1},{1,0},{2,3},{3,2},{4,5},{5,4},{6,7},{7,6},{8,9},{9,8},{10,11... | collective-permute-start | bytes 1179656 | tf_op jit(solution)/shard_map/ppermute | solution.py:656
  68.3 8.8 %collective-permute-start.12 = (bf16[256,768]{1,0:T(8,128)(2,1)S(1)}, bf16[256,768]{1,0:T(8,128)(2,1)S(1)}, u32[]{:S(2)}, u32[]{:S(2)}) collective-permute-start(bf16[256,768]{1,0:T(8,128)(2,1)S(1)} %collective-permute-done.11.refs_11_), channel_id=1, source_target_pairs={{0,1},{1,0},{2,3},{3,2},{4,5},{5,4},{6,7},{7,6},{8,9},{9,8},{10,11... | collective-permute-start | bytes 1179656 | tf_op jit(solution)/shard_map/ppermute | solution.py:656
  77.1 7.8 %collective-permute-start.14 = (bf16[256,768]{1,0:T(8,128)(2,1)S(1)}, bf16[256,768]{1,0:T(8,128)(2,1)S(1)}, u32[]{:S(2)}, u32[]{:S(2)}) collective-permute-start(bf16[256,768]{1,0:T(8,128)(2,1)S(1)} %collective-permute-done.13.refs_9_), channel_id=1, source_target_pairs={{0,1},{1,0},{2,3},{3,2},{4,5},{5,4},{6,7},{7,6},{8,9},{9,8},{10,11... | collective-permute-start | bytes 1179656 | tf_op jit(solution)/shard_map/ppermute | solution.py:656
  141.3 11.5 %collective-permute-start.17 = (bf16[256,768]{1,0:T(8,128)(2,1)S(1)}, bf16[256,768]{1,0:T(8,128)(2,1)S(1)}, u32[]{:S(2)}, u32[]{:S(2)}) collective-permute-start(bf16[256,768]{1,0:T(8,128)(2,1)S(1)} %get-tuple-element.142), channel_id=1, source_target_pairs={{0,2},{1,3},{2,0},{3,1},{4,6},{5,7},{6,4},{7,5},{8,10},{9,11},{10,... | collective-permute-start | bytes 1179656 | tf_op jit(solution)/shard_map/ppermute | solution.py:660
  143.1 12.0 %collective-permute-start.18 = (bf16[256,768]{1,0:T(8,128)(2,1)S(1)}, bf16[256,768]{1,0:T(8,128)(2,1)S(1)}, u32[]{:S(2)}, u32[]{:S(2)}) collective-permute-start(bf16[256,768]{1,0:T(8,128)(2,1)S(1)} %get-tuple-element.143), channel_id=1, source_target_pairs={{0,4},{1,5},{2,6},{3,7},{4,0},{5,1},{6,2},{7,3},{8,12},{9,13},{10,... | collective-permute-start | bytes 1179656 | tf_op jit(solution)/shard_map/ppermute | solution.py:664
  150.3 11.0 %collective-permute-start.19 = (bf16[256,768]{1,0:T(8,128)(2,1)S(1)}, bf16[256,768]{1,0:T(8,128)(2,1)S(1)}, u32[]{:S(2)}, u32[]{:S(2)}) collective-permute-start(bf16[256,768]{1,0:T(8,128)(2,1)S(1)} %get-tuple-element.146), channel_id=1, source_target_pairs={{0,2},{1,3},{2,0},{3,1},{4,6},{5,7},{6,4},{7,5},{8,10},{9,11},{10,... | collective-permute-start | bytes 1179656 | tf_op jit(solution)/shard_map/ppermute | solution.py:660
  150.9 12.4 %collective-permute-start.20 = (bf16[256,768]{1,0:T(8,128)(2,1)S(1)}, bf16[256,768]{1,0:T(8,128)(2,1)S(1)}, u32[]{:S(2)}, u32[]{:S(2)}) collective-permute-start(bf16[256,768]{1,0:T(8,128)(2,1)S(1)} %get-tuple-element.147), channel_id=1, source_target_pairs={{0,4},{1,5},{2,6},{3,7},{4,0},{5,1},{6,2},{7,3},{8,12},{9,13},{10,... | collective-permute-start | bytes 1179656 | tf_op jit(solution)/shard_map/ppermute | solution.py:664
  151.1 41.1 %collective-permute-start.67 = (bf16[256,3072]{1,0:T(8,128)(2,1)}, bf16[256,3072]{1,0:T(8,128)(2,1)S(1)}, u32[]{:S(2)}, u32[]{:S(2)}) collective-permute-start(bf16[256,3072]{1,0:T(8,128)(2,1)} %get-tuple-element.204.a_m), channel_id=1, source_target_pairs={{0,1},{1,0},{2,3},{3,2},{4,5},{5,4},{6,7},{7,6},{8,9},{9,8},{10,11... | collective-permute-start | bytes 4718600 | tf_op jit(solution)/shard_map/ppermute | solution.py:656
  152.8 47.5 %collective-permute-start.64 = (bf16[256,3072]{1,0:T(8,128)(2,1)}, bf16[256,3072]{1,0:T(8,128)(2,1)}, u32[]{:S(2)}, u32[]{:S(2)}) collective-permute-start(bf16[256,3072]{1,0:T(8,128)(2,1)} %get-tuple-element.201.g_m), channel_id=1, source_target_pairs={{0,1},{1,0},{2,3},{3,2},{4,5},{5,4},{6,7},{7,6},{8,9},{9,8},{10,11... | collective-permute-start | bytes 4718600 | tf_op jit(solution)/shard_map/ppermute | solution.py:656
  161.2 9.8 %collective-permute-start.23 = (bf16[256,768]{1,0:T(8,128)(2,1)S(1)}, bf16[256,768]{1,0:T(8,128)(2,1)S(1)}, u32[]{:S(2)}, u32[]{:S(2)}) collective-permute-start(bf16[256,768]{1,0:T(8,128)(2,1)S(1)} %get-tuple-element.152), channel_id=1, source_target_pairs={{0,2},{1,3},{2,0},{3,1},{4,6},{5,7},{6,4},{7,5},{8,10},{9,11},{10,... | collective-permute-start | bytes 1179656 | tf_op jit(solution)/shard_map/ppermute | solution.py:660
  161.3 11.2 %collective-permute-start.21 = (bf16[256,768]{1,0:T(8,128)(2,1)S(1)}, bf16[256,768]{1,0:T(8,128)(2,1)S(1)}, u32[]{:S(2)}, u32[]{:S(2)}) collective-permute-start(bf16[256,768]{1,0:T(8,128)(2,1)S(1)} %get-tuple-element.150), channel_id=1, source_target_pairs={{0,4},{1,5},{2,6},{3,7},{4,0},{5,1},{6,2},{7,3},{8,12},{9,13},{10,... | collective-permute-start | bytes 1179656 | tf_op jit(solution)/shard_map/ppermute | solution.py:664
  171.0 49.2 %collective-permute-start.56 = (bf16[256,3072]{1,0:T(8,128)(2,1)}, bf16[256,3072]{1,0:T(8,128)(2,1)}, u32[]{:S(2)}, u32[]{:S(2)}) collective-permute-start(bf16[256,3072]{1,0:T(8,128)(2,1)} %get-tuple-element.196.a_m), channel_id=1, source_target_pairs={{0,1},{1,0},{2,3},{3,2},{4,5},{5,4},{6,7},{7,6},{8,9},{9,8},{10,11... | collective-permute-start | bytes 4718600 | tf_op jit(solution)/shard_map/ppermute | solution.py:656
  175.5 24.3 %collective-permute-start.63 = (bf16[256,768]{1,0:T(8,128)(2,1)}, bf16[256,768]{1,0:T(8,128)(2,1)}, u32[]{:S(2)}, u32[]{:S(2)}) collective-permute-start(bf16[256,768]{1,0:T(8,128)(2,1)} %get-tuple-element.200.x_m), channel_id=1, source_target_pairs={{0,1},{1,0},{2,3},{3,2},{4,5},{5,4},{6,7},{7,6},{8,9},{9,8},{10,11... | collective-permute-start | bytes 1179656 | tf_op jit(solution)/shard_map/ppermute | solution.py:656
  178.8 28.0 %collective-permute-start.43 = (bf16[256,768]{1,0:T(8,128)(2,1)}, bf16[256,768]{1,0:T(8,128)(2,1)}, u32[]{:S(2)}, u32[]{:S(2)}) collective-permute-start(bf16[256,768]{1,0:T(8,128)(2,1)} %add.197.dkv.dkv_m), channel_id=1, source_target_pairs={{0,1},{1,0},{2,3},{3,2},{4,5},{5,4},{6,7},{7,6},{8,9},{9,8},{10,11... | collective-permute-start | bytes 1179656 | tf_op jit(solution)/shard_map/ppermute | solution.py:656
  193.4 17.8 %collective-permute-start.25 = (bf16[256,768]{1,0:T(8,128)(2,1)}, bf16[256,768]{1,0:T(8,128)(2,1)}, u32[]{:S(2)}, u32[]{:S(2)}) collective-permute-start(bf16[256,768]{1,0:T(8,128)(2,1)} %get-tuple-element.159.refs_1_.b_m), channel_id=1, source_target_pairs={{0,1},{1,0},{2,3},{3,2},{4,5},{5,4},{6,7},{7,6},{8,9},{9,8},{10,11... | collective-permute-start | bytes 1179656 | tf_op jit(solution)/shard_map/ppermute | solution.py:656
  200.4 101.6 %collective-permute-start.69 = (bf16[2,384,768]{2,1,0:T(8,128)(2,1)S(1)}, bf16[2,384,768]{2,1,0:T(8,128)(2,1)S(1)}, u32[]{:S(2)}, u32[]{:S(2)}) collective-permute-start(bf16[2,384,768]{2,1,0:T(8,128)(2,1)S(1)} %get-tuple-element.207), channel_id=1, source_target_pairs={{0,4},{1,5},{2,6},{3,7},{4,0},{5,1},{6,2},{7,3},{8,12},{9,13},{10,... | collective-permute-start | bytes 3538952 | tf_op jit(solution)/shard_map/ppermute | solution.py:664
  206.7 13.7 %collective-permute-start.57 = (bf16[256,768]{1,0:T(8,128)(2,1)S(1)}, bf16[256,768]{1,0:T(8,128)(2,1)S(1)}, u32[]{:S(2)}, u32[]{:S(2)}) collective-permute-start(bf16[256,768]{1,0:T(8,128)(2,1)S(1)} %copy-done.99), channel_id=1, source_target_pairs={{0,1},{1,0},{2,3},{3,2},{4,5},{5,4},{6,7},{7,6},{8,9},{9,8},{10,11... | collective-permute-start | bytes 1179656 | tf_op jit(solution)/shard_map/ppermute | solution.py:656
  210.7 48.9 %collective-permute-start.47 = (bf16[2,208,768]{2,1,0:T(8,128)(2,1)S(1)}, bf16[2,208,768]{2,1,0:T(8,128)(2,1)S(1)}, u32[]{:S(2)}, u32[]{:S(2)}) collective-permute-start(bf16[2,208,768]{2,1,0:T(8,128)(2,1)S(1)} %get-tuple-element.191), channel_id=1, source_target_pairs={{0,4},{1,5},{2,6},{3,7},{4,0},{5,1},{6,2},{7,3},{8,12},{9,13},{10,... | collective-permute-start | bytes 1916936 | tf_op jit(solution)/shard_map/ppermute | solution.py:664
  211.3 48.9 %collective-permute-start.45 = (bf16[2,208,768]{2,1,0:T(8,128)(2,1)S(1)}, bf16[2,208,768]{2,1,0:T(8,128)(2,1)S(1)}, u32[]{:S(2)}, u32[]{:S(2)}) collective-permute-start(bf16[2,208,768]{2,1,0:T(8,128)(2,1)S(1)} %get-tuple-element.189), channel_id=1, source_target_pairs={{0,2},{1,3},{2,0},{3,1},{4,6},{5,7},{6,4},{7,5},{8,10},{9,11},{10,... | collective-permute-start | bytes 1916936 | tf_op jit(solution)/shard_map/ppermute | solution.py:660
  220.2 15.8 %collective-permute-start.26 = (bf16[256,768]{1,0:T(8,128)(2,1)S(1)}, bf16[256,768]{1,0:T(8,128)(2,1)S(1)}, u32[]{:S(2)}, u32[]{:S(2)}) collective-permute-start(bf16[256,768]{1,0:T(8,128)(2,1)S(1)} %get-tuple-element.171), channel_id=1, source_target_pairs={{0,2},{1,3},{2,0},{3,1},{4,6},{5,7},{6,4},{7,5},{8,10},{9,11},{10,... | collective-permute-start | bytes 1179656 | tf_op jit(solution)/shard_map/ppermute | solution.py:660
  220.5 30.2 %collective-permute-start.27 = (bf16[256,768]{1,0:T(8,128)(2,1)S(1)}, bf16[256,768]{1,0:T(8,128)(2,1)S(1)}, u32[]{:S(2)}, u32[]{:S(2)}) collective-permute-start(bf16[256,768]{1,0:T(8,128)(2,1)S(1)} %get-tuple-element.172), channel_id=1, source_target_pairs={{0,4},{1,5},{2,6},{3,7},{4,0},{5,1},{6,2},{7,3},{8,12},{9,13},{10,... | collective-permute-start | bytes 1179656 | tf_op jit(solution)/shard_map/ppermute | solution.py:664
  236.1 22.0 %collective-permute-start.35 = (f32[16,768]{1,0:T(8,128)S(1)}, f32[16,768]{1,0:T(8,128)S(1)}, u32[]{:S(2)}, u32[]{:S(2)}) collective-permute-start(f32[16,768]{1,0:T(8,128)S(1)} %get-tuple-element.182.sums_m), channel_id=1, source_target_pairs={{0,1},{1,0},{2,3},{3,2},{4,5},{5,4},{6,7},{7,6},{8,9},{9,8},{10,11... | collective-permute-start | bytes 147464 | tf_op jit(solution)/shard_map/ppermute | solution.py:656
  250.6 10.6 %collective-permute-start.28 = (bf16[256,768]{1,0:T(8,128)(2,1)S(1)}, bf16[256,768]{1,0:T(8,128)(2,1)S(1)}, u32[]{:S(2)}, u32[]{:S(2)}) collective-permute-start(bf16[256,768]{1,0:T(8,128)(2,1)S(1)} %get-tuple-element.175), channel_id=1, source_target_pairs={{0,2},{1,3},{2,0},{3,1},{4,6},{5,7},{6,4},{7,5},{8,10},{9,11},{10,... | collective-permute-start | bytes 1179656 | tf_op jit(solution)/shard_map/ppermute | solution.py:660
  258.0 12.1 %collective-permute-start.29 = (bf16[256,768]{1,0:T(8,128)(2,1)S(1)}, bf16[256,768]{1,0:T(8,128)(2,1)S(1)}, u32[]{:S(2)}, u32[]{:S(2)}) collective-permute-start(bf16[256,768]{1,0:T(8,128)(2,1)S(1)} %get-tuple-element.176), channel_id=1, source_target_pairs={{0,4},{1,5},{2,6},{3,7},{4,0},{5,1},{6,2},{7,3},{8,12},{9,13},{10,... | collective-permute-start | bytes 1179656 | tf_op jit(solution)/shard_map/ppermute | solution.py:664
  259.6 12.1 %collective-permute-start.32 = (bf16[256,768]{1,0:T(8,128)(2,1)S(1)}, bf16[256,768]{1,0:T(8,128)(2,1)S(1)}, u32[]{:S(2)}, u32[]{:S(2)}) collective-permute-start(bf16[256,768]{1,0:T(8,128)(2,1)S(1)} %get-tuple-element.181), channel_id=1, source_target_pairs={{0,2},{1,3},{2,0},{3,1},{4,6},{5,7},{6,4},{7,5},{8,10},{9,11},{10,... | collective-permute-start | bytes 1179656 | tf_op jit(solution)/shard_map/ppermute | solution.py:660
  260.2 16.4 %collective-permute-start.30 = (bf16[256,768]{1,0:T(8,128)(2,1)S(1)}, bf16[256,768]{1,0:T(8,128)(2,1)S(1)}, u32[]{:S(2)}, u32[]{:S(2)}) collective-permute-start(bf16[256,768]{1,0:T(8,128)(2,1)S(1)} %get-tuple-element.179), channel_id=1, source_target_pairs={{0,4},{1,5},{2,6},{3,7},{4,0},{5,1},{6,2},{7,3},{8,12},{9,13},{10,... | collective-permute-start | bytes 1179656 | tf_op jit(solution)/shard_map/ppermute | solution.py:664
  261.3 49.2 %collective-permute-start.65 = (bf16[2,384,768]{2,1,0:T(8,128)(2,1)S(1)}, bf16[2,384,768]{2,1,0:T(8,128)(2,1)S(1)}, u32[]{:S(2)}, u32[]{:S(2)}) collective-permute-start(bf16[2,384,768]{2,1,0:T(8,128)(2,1)S(1)} %get-tuple-element.203), channel_id=1, source_target_pairs={{0,2},{1,3},{2,0},{3,1},{4,6},{5,7},{6,4},{7,5},{8,10},{9,11},{10,... | collective-permute-start | bytes 3538952 | tf_op jit(solution)/shard_map/ppermute | solution.py:660
  270.2 47.6 %collective-permute-start.53 = (bf16[256,3072]{1,0:T(8,128)(2,1)S(1)}, bf16[256,3072]{1,0:T(8,128)(2,1)S(1)}, u32[]{:S(2)}, u32[]{:S(2)}) collective-permute-start(bf16[256,3072]{1,0:T(8,128)(2,1)S(1)} %copy-done.69), channel_id=1, source_target_pairs={{0,1},{1,0},{2,3},{3,2},{4,5},{5,4},{6,7},{7,6},{8,9},{9,8},{10,11... | collective-permute-start | bytes 4718600 | tf_op jit(solution)/shard_map/ppermute | solution.py:656
  271.7 29.9 %collective-permute-start.48 = (bf16[208,768]{1,0:T(8,128)(2,1)S(1)}, bf16[208,768]{1,0:T(8,128)(2,1)S(1)}, u32[]{:S(2)}, u32[]{:S(2)}) collective-permute-start(bf16[208,768]{1,0:T(8,128)(2,1)S(1)} %fusion.12), channel_id=1, source_target_pairs={{0,2},{1,3},{2,0},{3,1},{4,6},{5,7},{6,4},{7,5},{8,10},{9,11},{10,... | collective-permute-start | bytes 958472 | tf_op jit(solution)/shard_map/ppermute | solution.py:660
  276.6 25.0 %collective-permute-start.46 = (bf16[208,768]{1,0:T(8,128)(2,1)S(1)}, bf16[208,768]{1,0:T(8,128)(2,1)S(1)}, u32[]{:S(2)}, u32[]{:S(2)}) collective-permute-start(bf16[208,768]{1,0:T(8,128)(2,1)S(1)} %fusion.15), channel_id=1, source_target_pairs={{0,4},{1,5},{2,6},{3,7},{4,0},{5,1},{6,2},{7,3},{8,12},{9,13},{10,... | collective-permute-start | bytes 958472 | tf_op jit(solution)/shard_map/ppermute | solution.py:664
  303.4 13.8 %collective-permute-start.52 = (bf16[256,768]{1,0:T(8,128)(2,1)S(1)}, bf16[256,768]{1,0:T(8,128)(2,1)S(1)}, u32[]{:S(2)}, u32[]{:S(2)}) collective-permute-start(bf16[256,768]{1,0:T(8,128)(2,1)S(1)} %copy-done.93), channel_id=1, source_target_pairs={{0,1},{1,0},{2,3},{3,2},{4,5},{5,4},{6,7},{7,6},{8,9},{9,8},{10,11... | collective-permute-start | bytes 1179656 | tf_op jit(solution)/shard_map/ppermute | solution.py:656
  303.8 57.1 %collective-permute-start.58 = (bf16[2,384,768]{2,1,0:T(8,128)(2,1)S(1)}, bf16[2,384,768]{2,1,0:T(8,128)(2,1)S(1)}, u32[]{:S(2)}, u32[]{:S(2)}) collective-permute-start(bf16[2,384,768]{2,1,0:T(8,128)(2,1)S(1)} %get-tuple-element.199), channel_id=1, source_target_pairs={{0,4},{1,5},{2,6},{3,7},{4,0},{5,1},{6,2},{7,3},{8,12},{9,13},{10,... | collective-permute-start | bytes 3538952 | tf_op jit(solution)/shard_map/ppermute | solution.py:664
  305.5 9.3 %collective-permute-start.49 = (bf16[208,768]{1,0:T(8,128)(2,1)S(1)}, bf16[208,768]{1,0:T(8,128)(2,1)S(1)}, u32[]{:S(2)}, u32[]{:S(2)}) collective-permute-start(bf16[208,768]{1,0:T(8,128)(2,1)S(1)} %broadcast_select_fusion.6), channel_id=1, source_target_pairs={{0,8},{8,0},{16,24},{24,16},{1,9},{9,1},{17,25},{25,17},{2,10},{10... | collective-permute-start | bytes 958472 | tf_op jit(solution)/shard_map/ppermute | solution.py:668
  310.5 35.9 %collective-permute-start.38 = (bf16[2,208,768]{2,1,0:T(8,128)(2,1)S(1)}, bf16[2,208,768]{2,1,0:T(8,128)(2,1)S(1)}, u32[]{:S(2)}, u32[]{:S(2)}) collective-permute-start(bf16[2,208,768]{2,1,0:T(8,128)(2,1)S(1)} %get-tuple-element.186), channel_id=1, source_target_pairs={{0,4},{1,5},{2,6},{3,7},{4,0},{5,1},{6,2},{7,3},{8,12},{9,13},{10,... | collective-permute-start | bytes 1916936 | tf_op jit(solution)/shard_map/ppermute | solution.py:664
  314.8 35.9 %collective-permute-start.36 = (bf16[2,208,768]{2,1,0:T(8,128)(2,1)S(1)}, bf16[2,208,768]{2,1,0:T(8,128)(2,1)S(1)}, u32[]{:S(2)}, u32[]{:S(2)}) collective-permute-start(bf16[2,208,768]{2,1,0:T(8,128)(2,1)S(1)} %get-tuple-element.184), channel_id=1, source_target_pairs={{0,2},{1,3},{2,0},{3,1},{4,6},{5,7},{6,4},{7,5},{8,10},{9,11},{10,... | collective-permute-start | bytes 1916936 | tf_op jit(solution)/shard_map/ppermute | solution.py:660
  317.2 35.9 %collective-permute-start.70 = (bf16[384,768]{1,0:T(8,128)(2,1)S(1)}, bf16[384,768]{1,0:T(8,128)(2,1)S(1)}, u32[]{:S(2)}, u32[]{:S(2)}) collective-permute-start(bf16[384,768]{1,0:T(8,128)(2,1)S(1)} %fusion), channel_id=1, source_target_pairs={{0,2},{1,3},{2,0},{3,1},{4,6},{5,7},{6,4},{7,5},{8,10},{9,11},{10,... | collective-permute-start | bytes 1769480 | tf_op jit(solution)/shard_map/ppermute | solution.py:660
  317.8 40.4 %collective-permute-start.66 = (bf16[384,768]{1,0:T(8,128)(2,1)S(1)}, bf16[384,768]{1,0:T(8,128)(2,1)S(1)}, u32[]{:S(2)}, u32[]{:S(2)}) collective-permute-start(bf16[384,768]{1,0:T(8,128)(2,1)S(1)} %fusion.3), channel_id=1, source_target_pairs={{0,4},{1,5},{2,6},{3,7},{4,0},{5,1},{6,2},{7,3},{8,12},{9,13},{10,... | collective-permute-start | bytes 1769480 | tf_op jit(solution)/shard_map/ppermute | solution.py:664
  346.3 19.4 %collective-permute-start.50 = (bf16[208,768]{1,0:T(8,128)(2,1)}, bf16[208,768]{1,0:T(8,128)(2,1)}, u32[]{:S(2)}, u32[]{:S(2)}) collective-permute-start(bf16[208,768]{1,0:T(8,128)(2,1)} %select_add_fusion.2), channel_id=1, source_target_pairs={{0,24},{24,0},{8,16},{16,8},{1,25},{25,1},{9,17},{17,9},{2,26},{26... | collective-permute-start | bytes 958472 | tf_op jit(solution)/shard_map/ppermute | solution.py:668
  350.7 43.0 %collective-permute-start.54 = (bf16[2,384,768]{2,1,0:T(8,128)(2,1)}, bf16[2,384,768]{2,1,0:T(8,128)(2,1)}, u32[]{:S(2)}, u32[]{:S(2)}) collective-permute-start(bf16[2,384,768]{2,1,0:T(8,128)(2,1)} %get-tuple-element.195), channel_id=1, source_target_pairs={{0,2},{1,3},{2,0},{3,1},{4,6},{5,7},{6,4},{7,5},{8,10},{9,11},{10,... | collective-permute-start | bytes 3538952 | tf_op jit(solution)/shard_map/ppermute | solution.py:660
  353.1 33.6 %collective-permute-start.39 = (bf16[208,768]{1,0:T(8,128)(2,1)}, bf16[208,768]{1,0:T(8,128)(2,1)}, u32[]{:S(2)}, u32[]{:S(2)}) collective-permute-start(bf16[208,768]{1,0:T(8,128)(2,1)} %fusion.18), channel_id=1, source_target_pairs={{0,2},{1,3},{2,0},{3,1},{4,6},{5,7},{6,4},{7,5},{8,10},{9,11},{10,... | collective-permute-start | bytes 958472 | tf_op jit(solution)/shard_map/ppermute | solution.py:660
  358.2 28.6 %collective-permute-start.37 = (bf16[208,768]{1,0:T(8,128)(2,1)}, bf16[208,768]{1,0:T(8,128)(2,1)}, u32[]{:S(2)}, u32[]{:S(2)}) collective-permute-start(bf16[208,768]{1,0:T(8,128)(2,1)} %fusion.21), channel_id=1, source_target_pairs={{0,4},{1,5},{2,6},{3,7},{4,0},{5,1},{6,2},{7,3},{8,12},{9,13},{10,... | collective-permute-start | bytes 958472 | tf_op jit(solution)/shard_map/ppermute | solution.py:664
  362.0 28.3 %collective-permute-start.71 = (bf16[384,768]{1,0:T(8,128)(2,1)}, bf16[384,768]{1,0:T(8,128)(2,1)}, u32[]{:S(2)}, u32[]{:S(2)}) collective-permute-start(bf16[384,768]{1,0:T(8,128)(2,1)} %broadcast_select_fusion.1), channel_id=1, source_target_pairs={{0,8},{8,0},{16,24},{24,16},{1,9},{9,1},{17,25},{25,17},{2,10},{10... | collective-permute-start | bytes 1769480 | tf_op jit(solution)/shard_map/ppermute | solution.py:668
  365.7 65.2 %collective-permute-start.59 = (bf16[384,768]{1,0:T(8,128)(2,1)}, bf16[384,768]{1,0:T(8,128)(2,1)}, u32[]{:S(2)}, u32[]{:S(2)}) collective-permute-start(bf16[384,768]{1,0:T(8,128)(2,1)} %fusion.6), channel_id=1, source_target_pairs={{0,2},{1,3},{2,0},{3,1},{4,6},{5,7},{6,4},{7,5},{8,10},{9,11},{10,... | collective-permute-start | bytes 1769480 | tf_op jit(solution)/shard_map/ppermute | solution.py:660
  386.8 31.7 %collective-permute-start.51 = (bf16[208,768]{1,0:T(8,128)(2,1)S(1)}, bf16[208,768]{1,0:T(8,128)(2,1)S(1)}, u32[]{:S(2)}, u32[]{:S(2)}) collective-permute-start(bf16[208,768]{1,0:T(8,128)(2,1)S(1)} %add.224), channel_id=1, source_target_pairs={{0,8},{8,0},{16,24},{24,16},{1,9},{9,1},{17,25},{25,17},{2,10},{10... | collective-permute-start | bytes 958472 | tf_op jit(solution)/shard_map/ppermute | solution.py:668
  388.2 25.4 %collective-permute-start.40 = (bf16[208,768]{1,0:T(8,128)(2,1)S(1)}, bf16[208,768]{1,0:T(8,128)(2,1)S(1)}, u32[]{:S(2)}, u32[]{:S(2)}) collective-permute-start(bf16[208,768]{1,0:T(8,128)(2,1)S(1)} %broadcast_select_fusion.9), channel_id=1, source_target_pairs={{0,8},{8,0},{16,24},{24,16},{1,9},{9,1},{17,25},{25,17},{2,10},{10... | collective-permute-start | bytes 958472 | tf_op jit(solution)/shard_map/ppermute | solution.py:668
  393.4 27.1 %collective-permute-start.72 = (bf16[384,768]{1,0:T(8,128)(2,1)}, bf16[384,768]{1,0:T(8,128)(2,1)}, u32[]{:S(2)}, u32[]{:S(2)}) collective-permute-start(bf16[384,768]{1,0:T(8,128)(2,1)} %select_add_fusion), channel_id=1, source_target_pairs={{0,24},{24,0},{8,16},{16,8},{1,25},{25,1},{9,17},{17,9},{2,26},{26... | collective-permute-start | bytes 1769480 | tf_op jit(solution)/shard_map/ppermute | solution.py:668
  395.8 35.1 %collective-permute-start.55 = (bf16[384,768]{1,0:T(8,128)(2,1)}, bf16[384,768]{1,0:T(8,128)(2,1)}, u32[]{:S(2)}, u32[]{:S(2)}) collective-permute-start(bf16[384,768]{1,0:T(8,128)(2,1)} %fusion.9), channel_id=1, source_target_pairs={{0,4},{1,5},{2,6},{3,7},{4,0},{5,1},{6,2},{7,3},{8,12},{9,13},{10,... | collective-permute-start | bytes 1769480 | tf_op jit(solution)/shard_map/ppermute | solution.py:664
  415.6 12.6 %collective-permute-start.41 = (bf16[208,768]{1,0:T(8,128)(2,1)}, bf16[208,768]{1,0:T(8,128)(2,1)}, u32[]{:S(2)}, u32[]{:S(2)}) collective-permute-start(bf16[208,768]{1,0:T(8,128)(2,1)} %select_add_fusion.3), channel_id=1, source_target_pairs={{0,24},{24,0},{8,16},{16,8},{1,25},{25,1},{9,17},{17,9},{2,26},{26... | collective-permute-start | bytes 958472 | tf_op jit(solution)/shard_map/ppermute | solution.py:668
  422.0 58.0 %collective-permute-start.73 = (bf16[384,768]{1,0:T(8,128)(2,1)S(1)}, bf16[384,768]{1,0:T(8,128)(2,1)}, u32[]{:S(2)}, u32[]{:S(2)}) collective-permute-start(bf16[384,768]{1,0:T(8,128)(2,1)S(1)} %add.250), channel_id=1, source_target_pairs={{0,8},{8,0},{16,24},{24,16},{1,9},{9,1},{17,25},{25,17},{2,10},{10... | collective-permute-start | bytes 1769480 | tf_op jit(solution)/shard_map/ppermute | solution.py:668
  429.4 17.2 %collective-permute-start.42 = (bf16[208,768]{1,0:T(8,128)(2,1)S(1)}, bf16[208,768]{1,0:T(8,128)(2,1)S(1)}, u32[]{:S(2)}, u32[]{:S(2)}) collective-permute-start(bf16[208,768]{1,0:T(8,128)(2,1)S(1)} %add.212), channel_id=1, source_target_pairs={{0,8},{8,0},{16,24},{24,16},{1,9},{9,1},{17,25},{25,17},{2,10},{10... | collective-permute-start | bytes 958472 | tf_op jit(solution)/shard_map/ppermute | solution.py:668
  433.3 22.2 %collective-permute-start.60 = (bf16[384,768]{1,0:T(8,128)(2,1)}, bf16[384,768]{1,0:T(8,128)(2,1)}, u32[]{:S(2)}, u32[]{:S(2)}) collective-permute-start(bf16[384,768]{1,0:T(8,128)(2,1)} %broadcast_select_fusion.3), channel_id=1, source_target_pairs={{0,8},{8,0},{16,24},{24,16},{1,9},{9,1},{17,25},{25,17},{2,10},{10... | collective-permute-start | bytes 1769480 | tf_op jit(solution)/shard_map/ppermute | solution.py:668
  457.5 11.9 %collective-permute-start.61 = (bf16[384,768]{1,0:T(8,128)(2,1)S(1)}, bf16[384,768]{1,0:T(8,128)(2,1)S(1)}, u32[]{:S(2)}, u32[]{:S(2)}) collective-permute-start(bf16[384,768]{1,0:T(8,128)(2,1)S(1)} %select_add_fusion.1), channel_id=1, source_target_pairs={{0,24},{24,0},{8,16},{16,8},{1,25},{25,1},{9,17},{17,9},{2,26},{26... | collective-permute-start | bytes 1769480 | tf_op jit(solution)/shard_map/ppermute | solution.py:668
  469.6 18.6 %collective-permute-start.62 = (bf16[384,768]{1,0:T(8,128)(2,1)S(1)}, bf16[384,768]{1,0:T(8,128)(2,1)S(1)}, u32[]{:S(2)}, u32[]{:S(2)}) collective-permute-start(bf16[384,768]{1,0:T(8,128)(2,1)S(1)} %add.238), channel_id=1, source_target_pairs={{0,8},{8,0},{16,24},{24,16},{1,9},{9,1},{17,25},{25,17},{2,10},{10... | collective-permute-start | bytes 1769480 | tf_op jit(solution)/shard_map/ppermute | solution.py:668
  (142 other events, 1761.8 us)
